TPU v7x, 32 devices: a whole 2x2x4 slice. The times are simulated.
32 devices in a mesh: fsdp: 8 (over z, y), tp: 4 (over x, core).
Axes of the slice: x: 2, y: 2, z: 4, core: 2. Of those that a mesh axis runs over, the one named last changes fastest.
Arguments:
- llm_query: bfloat16 [8, 64, 8192], P('fsdp', None, 'tp'), may hold values from -15 to 15
- llm_kv: bfloat16 [8, 2, 320, 1024], P('fsdp', None, 'tp'), may hold values from -15 to 15
- connector: bfloat16 [8192, 6144], P('tp', 'fsdp'), may hold values from -0.75 to 0.75
- self_query: bfloat16 [8, 2, 1024, 3072], P('fsdp', None, 'tp'), may hold values from -15 to 15
- self_key: bfloat16 [8, 2, 1024, 3072], P('fsdp', None, 'tp'), may hold values from -15 to 15
- latent_value: bfloat16 [8, 2, 1024, 3072], P('fsdp', None, 'tp'), may hold values from -6 to 6
- cotangent: bfloat16 [8, 2, 1024, 3072], P('fsdp', None, 'tp'), may hold values from -6 to 6
Outputs:
- latent_out: bfloat16 [8, 2, 1024, 3072], P('fsdp', None, 'tp')
- self_grad: bfloat16 [8, 2, 1024, 3072], P('fsdp', None, 'tp')
- context_grad: bfloat16 [8, 2, 64, 3072], P('fsdp', None, None, 'tp')
All inputs are finite; a program needn't handle non-finite values.
Results may differ from a plain program's by a relative error of at most 0.015.
Values may be sent and summed in bfloat16 or wider, within the bound.
A program may use at most 128 MiB of HBM per device.

v0:
```python
import jax
import jax.numpy as jnp
from jax import lax
from jax.sharding import PartitionSpec as P

HEAD_SIZE = 128
LLM_HEADS = 64
LLM_KV = 8
DENOISER_HEADS = 24
QUERY_TOKENS = 64
LATENT_TOKENS = 1024
SAMPLE_COUNT = 2
PROMPT = 256


norm_eps = 1e-06


def softmax_rows(scores, axis_index):
    top_value = jnp.max(scores, axis=axis_index, keepdims=True)
    exp_terms = jnp.exp(scores - top_value)
    return exp_terms / jnp.sum(exp_terms, axis=axis_index, keepdims=True)


def llm_hidden(llm_query, llm_kv):
    whole_kv = lax.all_gather(llm_kv, "tp", axis=2, tiled=True)
    query_heads = llm_query.shape[2] // HEAD_SIZE
    group_total = LLM_HEADS // LLM_KV
    kv_heads = max(query_heads // group_total, 1)
    group_size = query_heads // kv_heads
    first_kv = lax.axis_index("tp") * query_heads // group_total
    local_kv = lax.dynamic_slice_in_dim(whole_kv, first_kv * HEAD_SIZE, kv_heads * HEAD_SIZE, 3)
    positions = local_kv.shape[2]
    queries = llm_query[0].reshape(QUERY_TOKENS, kv_heads, group_size, HEAD_SIZE)
    keys_all = local_kv[0, 0].reshape(positions, kv_heads, HEAD_SIZE)
    values_all = local_kv[0, 1].reshape(positions, kv_heads, HEAD_SIZE)
    scores = jnp.einsum(
        "qkgd,pkd->kgqp", queries, keys_all, preferred_element_type=jnp.float32
    ) * HEAD_SIZE ** (-0.5)
    allowed = jnp.arange(positions)[None, :] <= PROMPT + jnp.arange(QUERY_TOKENS)[:, None]
    scores = jnp.where(allowed, scores, -1e30)
    weights = softmax_rows(scores, 3).astype(jnp.bfloat16)
    mixed_heads = jnp.einsum(
        "kgqp,pkd->qkgd", weights, values_all, preferred_element_type=jnp.float32
    )
    return mixed_heads.astype(jnp.bfloat16).reshape(QUERY_TOKENS, query_heads * HEAD_SIZE)


def rms_inverse(incoming_values):
    return lax.rsqrt(jnp.mean(incoming_values * incoming_values, axis=-1, keepdims=True) + norm_eps)


def norm_back(grad_normed, normed, inverse):
    return inverse * (grad_normed - normed * jnp.mean(grad_normed * normed, axis=-1, keepdims=True))


def cross_core(latent_heads, condition_keys, condition_values, gradient_heads):
    score_scale = HEAD_SIZE ** (-0.5)
    self_float = latent_heads.astype(jnp.float32)
    query_inverse = rms_inverse(self_float)
    query_normed = self_float * query_inverse
    query_round = query_normed.astype(jnp.bfloat16)
    key_float = condition_keys.astype(jnp.float32)
    key_inverse = rms_inverse(key_float)
    key_normed = key_float * key_inverse
    key_round = key_normed.astype(jnp.bfloat16)
    scores = (
        jnp.einsum("hrd,chd->hcr", query_round, key_round, preferred_element_type=jnp.float32)
        * score_scale
    )
    exp_terms = jnp.exp(scores)
    attention_weights = exp_terms / jnp.sum(exp_terms, axis=1, keepdims=True)
    weights_round = attention_weights.astype(jnp.bfloat16)
    cross_out = jnp.einsum(
        "hcr,chd->hrd", weights_round, condition_values, preferred_element_type=jnp.float32
    )
    total_heads = self_float + cross_out
    value_gradient = jnp.einsum(
        "hcr,hrd->chd", weights_round, gradient_heads, preferred_element_type=jnp.float32
    )
    weight_grad = jnp.einsum(
        "hrd,chd->hcr", gradient_heads, condition_values, preferred_element_type=jnp.float32
    )
    delta_rows = jnp.sum(attention_weights * weight_grad, axis=1, keepdims=True)
    score_grad = (attention_weights * (weight_grad - delta_rows) * score_scale).astype(jnp.bfloat16)
    query_grad = jnp.einsum(
        "hcr,chd->hrd", score_grad, key_round, preferred_element_type=jnp.float32
    )
    key_grad_normed = jnp.einsum(
        "hcr,hrd->chd", score_grad, query_round, preferred_element_type=jnp.float32
    )
    self_grad = gradient_heads.astype(jnp.float32) + norm_back(
        query_grad, query_normed, query_inverse
    )
    key_gradient = norm_back(key_grad_normed, key_normed, key_inverse)
    return (total_heads, self_grad, key_gradient, value_gradient)


def self_attention(head_query, head_key, head_value):
    block_rows = min(512, LATENT_TOKENS)
    pieces = []
    for block_start in range(0, LATENT_TOKENS, block_rows):
        block_query = head_query[:, block_start : block_start + block_rows]
        scores = jnp.einsum(
            "iqd,ikd->iqk", block_query, head_key, preferred_element_type=jnp.float32
        ) * HEAD_SIZE ** (-0.5)
        weights = softmax_rows(scores, 2).astype(jnp.bfloat16)
        pieces.append(
            jnp.einsum(
                "iqk,ikd->iqd", weights, head_value, preferred_element_type=jnp.float32
            ).astype(jnp.bfloat16)
        )
    return jnp.concatenate(pieces, axis=1)


def shards(llm_query, llm_kv, connector, self_query, self_key, latent_value, cotangent):
    hidden = llm_hidden(llm_query, llm_kv)
    every_hidden = lax.all_gather(hidden, "fsdp", axis=0, tiled=True)
    partial_kv = jnp.dot(every_hidden, connector, preferred_element_type=jnp.float32)
    summed_kv = lax.psum(partial_kv, "tp").astype(jnp.bfloat16)
    condition_tokens = lax.all_to_all(summed_kv, "fsdp", split_axis=0, concat_axis=1, tiled=True)
    device_rows = self_query.shape[2]

    def heads_first(incoming_values):
        return (
            incoming_values[0]
            .reshape(SAMPLE_COUNT, device_rows, DENOISER_HEADS, HEAD_SIZE)
            .transpose(0, 2, 1, 3)
            .reshape(SAMPLE_COUNT * DENOISER_HEADS, device_rows, HEAD_SIZE)
        )

    head_query, head_key, head_value = (
        lax.all_to_all(heads_first(self_query), "tp", split_axis=0, concat_axis=1, tiled=True),
        lax.all_to_all(heads_first(self_key), "tp", split_axis=0, concat_axis=1, tiled=True),
        lax.all_to_all(heads_first(latent_value), "tp", split_axis=0, concat_axis=1, tiled=True),
    )
    head_out = self_attention(head_query, head_key, head_value)
    sequence_output = lax.all_to_all(head_out, "tp", split_axis=1, concat_axis=0, tiled=True)
    gathered_rows = SAMPLE_COUNT * device_rows
    latent_heads = (
        sequence_output.reshape(SAMPLE_COUNT, DENOISER_HEADS, device_rows, HEAD_SIZE)
        .transpose(1, 0, 2, 3)
        .reshape(DENOISER_HEADS, gathered_rows, HEAD_SIZE)
    )
    gradient_heads = (
        cotangent[0]
        .reshape(SAMPLE_COUNT, device_rows, DENOISER_HEADS, HEAD_SIZE)
        .transpose(2, 0, 1, 3)
        .reshape(DENOISER_HEADS, gathered_rows, HEAD_SIZE)
    )
    model_width = DENOISER_HEADS * HEAD_SIZE
    condition_keys = condition_tokens[:, :model_width].reshape(
        QUERY_TOKENS, DENOISER_HEADS, HEAD_SIZE
    )
    condition_values = condition_tokens[:, model_width:].reshape(
        QUERY_TOKENS, DENOISER_HEADS, HEAD_SIZE
    )
    total_heads, grad_total, key_gradient, value_gradient = cross_core(
        latent_heads, condition_keys, condition_values, gradient_heads
    )

    def to_rows(incoming_values):
        return (
            incoming_values.reshape(DENOISER_HEADS, SAMPLE_COUNT, device_rows, HEAD_SIZE)
            .transpose(1, 2, 0, 3)
            .reshape(1, SAMPLE_COUNT, device_rows, DENOISER_HEADS * HEAD_SIZE)
            .astype(jnp.bfloat16)
        )

    latent_out = to_rows(total_heads)
    self_grad = to_rows(grad_total)
    partial_grad = jnp.stack(
        [
            key_gradient.reshape(QUERY_TOKENS, model_width),
            value_gradient.reshape(QUERY_TOKENS, model_width),
        ]
    )[None]
    context_grad = lax.psum_scatter(
        partial_grad.astype(jnp.bfloat16), "tp", scatter_dimension=3, tiled=True
    )
    return (latent_out, self_grad, context_grad)


def solution(mesh):
    placed = (
        P("fsdp", None, "tp"),
        P("fsdp", None, "tp", None),
        P("tp", "fsdp"),
        P("fsdp", None, "tp", None),
        P("fsdp", None, "tp", None),
        P("fsdp", None, "tp", None),
        P("fsdp", None, "tp", None),
    )
    return jax.shard_map(
        shards,
        mesh=mesh,
        in_specs=placed,
        out_specs=(
            P("fsdp", None, "tp", None),
            P("fsdp", None, "tp", None),
            P("fsdp", None, None, "tp"),
        ),
        check_vma=False,
    )
```

profile of v0, /device:TPU:0, one launch (start us, length us, event | category | flops | bytes accessed | tf_op | source)
XLA Modules:
  0.0 363.2 jit_solution(17981469112121784243)
XLA Ops:
  7.2 4.8 %copy.150 = bf16[1,2,256,3072]{2,3,1,0:T(8,128)(2,1)} copy(bf16[1,2,256,3072]{3,2,1,0:T(8,128)(2,1)} %param.11) | data formatting | bytes 6291456 | tf_op args[4]
  16.6 4.6 %all-to-all-start.1 = ((bf16[48,256,128]{2,1,0:T(8,128)(2,1)}), bf16[48,256,128]{2,1,0:T(8,128)(2,1)}, u32[]{:S(2)}, u32[]{:S(2)}) async-start(bf16[48,256,128]{2,1,0:T(8,128)(2,1)} %bitcast.148), calls=%async_computation.1 | async-start | bytes 6291456 | tf_op jit(solution)/shard_map/all_to_all | solution.py:134
  22.0 4.6 %copy.147 = bf16[1,2,256,3072]{2,3,1,0:T(8,128)(2,1)} copy(bf16[1,2,256,3072]{3,2,1,0:T(8,128)(2,1)} %param.10) | data formatting | bytes 6291456 | tf_op args[3]
  26.6 4.7 %copy.148 = bf16[2,24,256,128]{3,2,1,0:T(8,128)(2,1)} copy(bf16[2,24,256,128]{2,3,1,0:T(8,128)(2,1)} %bitcast.150) | data formatting | bytes 6291456 | tf_op jit(solution)/shard_map/transpose | solution.py:128
  31.3 34.6 %all-to-all-done.1 = bf16[48,256,128]{2,1,0:T(8,128)(2,1)} async-done(((bf16[48,256,128]{2,1,0:T(8,128)(2,1)}), bf16[48,256,128]{2,1,0:T(8,128)(2,1)}, u32[]{:S(2)}, u32[]{:S(2)}) %all-to-all-start.1) | async-done | bytes 3145760 | tf_op jit(solution)/shard_map/all_to_all | solution.py:134
  75.3 4.7 %copy.154 = bf16[2,24,256,128]{3,2,1,0:T(8,128)(2,1)} copy(bf16[2,24,256,128]{2,3,1,0:T(8,128)(2,1)} %bitcast.151) | data formatting | bytes 6291456 | tf_op jit(solution)/shard_map/transpose | solution.py:128
  92.9 14.6 %all-to-all-done = bf16[48,256,128]{2,1,0:T(8,128)(2,1)} async-done(((bf16[48,256,128]{2,1,0:T(8,128)(2,1)}), bf16[48,256,128]{2,1,0:T(8,128)(2,1)}, u32[]{:S(2)}, u32[]{:S(2)}) %all-to-all-start) | async-done | bytes 3145760 | tf_op jit(solution)/shard_map/all_to_all | solution.py:133
  107.6 4.8 %all-to-all-start.2 = ((bf16[48,256,128]{2,1,0:T(8,128)(2,1)}), bf16[48,256,128]{2,1,0:T(8,128)(2,1)}, u32[]{:S(2)}, u32[]{:S(2)}) async-start(bf16[48,256,128]{2,1,0:T(8,128)(2,1)} %bitcast.147), calls=%async_computation.2 | async-start | bytes 6291456 | tf_op jit(solution)/shard_map/all_to_all | solution.py:135
  116.3 13.8 %fusion.106 = (f32[12,512]{1,0:T(8,128)S(1)}, f32[12,512,1024]{2,1,0:T(8,128)}) fusion(bf16[12,1024,128]{2,1,0:T(8,128)(2,1)} %bitcast.155, bf16[12,1024,128]{2,1,0:T(8,128)(2,1)} %bitcast.159), kind=kOutput, calls=%fused_computation.95 | convolution fusion | flops 1629488128 | bytes 29908992 | tf_op jit(solution)/shard_map/sub | solution.py:21
  130.1 13.7 %fusion.111 = (f32[12,512]{1,0:T(8,128)S(1)}, f32[12,512,1024]{2,1,0:T(8,128)}) fusion(bf16[12,1024,128]{2,1,0:T(8,128)(2,1)} %bitcast.156, bf16[12,1024,128]{2,1,0:T(8,128)(2,1)} %bitcast.160), kind=kOutput, calls=%fused_computation.96 | convolution fusion | flops 1629488128 | bytes 29908992 | tf_op jit(solution)/shard_map/sub | solution.py:21
  143.8 5.6 %all-to-all-done.2 = bf16[48,256,128]{2,1,0:T(8,128)(2,1)} async-done(((bf16[48,256,128]{2,1,0:T(8,128)(2,1)}), bf16[48,256,128]{2,1,0:T(8,128)(2,1)}, u32[]{:S(2)}, u32[]{:S(2)}) %all-to-all-start.2) | async-done | bytes 3145760 | tf_op jit(solution)/shard_map/all_to_all | solution.py:135
  151.6 10.1 %fusion.33 = bf16[12,512,128]{2,1,0:T(8,128)(2,1)S(1)} fusion(bf16[12,1024,128]{2,1,0:T(8,128)(2,1)S(1)} %bitcast.157, f32[12,512,1024]{2,1,0:T(8,128)} %get-tuple-element.11, f32[12,512]{1,0:T(8,128)S(1)} %get-tuple-element.10), kind=kOutput, calls=%fused_computation.37 | convolution fusion | flops 1623982080 | bytes 29908992 | tf_op jit(solution)/shard_map/iqk,ikd->iqd/dot_general | solution.py:109
  161.7 10.3 %fusion.34 = bf16[12,512,128]{2,1,0:T(8,128)(2,1)S(1)} fusion(bf16[12,1024,128]{2,1,0:T(8,128)(2,1)S(1)} %bitcast.158, f32[12,512,1024]{2,1,0:T(8,128)} %get-tuple-element.13, f32[12,512]{1,0:T(8,128)S(1)} %get-tuple-element.12), kind=kOutput, calls=%fused_computation.38 | convolution fusion | flops 1623982080 | bytes 29908992 | tf_op jit(solution)/shard_map/iqk,ikd->iqd/dot_general | solution.py:109
  176.4 4.9 %all-to-all-start.3 = ((bf16[12,1024,128]{2,0,1:T(8,128)(2,1)}), bf16[12,1024,128]{2,0,1:T(8,128)(2,1)}, u32[]{:S(2)}, u32[]{:S(2)}) async-start(bf16[12,1024,128]{2,0,1:T(8,128)(2,1)} %copy.156), calls=%async_computation.3 | async-start | bytes 8388608 | tf_op jit(solution)/shard_map/all_to_all | solution.py:138
  191.0 65.9 %all-reduce.1 = bf16[512,768]{1,0:T(8,128)(2,1)} all-reduce(f32[512,768]{1,0:T(8,128)} %fusion.125), channel_id=1, replica_groups=mesh['fsdp'=8,'tp'=4] {'tp'}, use_global_device_ids=true, to_apply=%region_6.7 | all-reduce | flops 393216 | bytes 2359296 | tf_op jit(solution)/shard_map/psum | solution.py:120
  257.0 6.6 %all-to-all-start.4 = ((bf16[8,64,768]{2,1,0:T(8,128)(2,1)}), bf16[8,64,768]{2,1,0:T(8,128)(2,1)}, u32[]{:S(2)}, u32[]{:S(2)}) async-start(bf16[8,64,768]{2,1,0:T(8,128)(2,1)} %bitcast.163), calls=%async_computation.4 | async-start | bytes 1572864 | tf_op jit(solution)/shard_map/all_to_all | solution.py:121
  273.0 6.5 %fusion.16 = bf16[24,512,128]{2,1,0:T(8,128)(2,1)} fusion(f32[24,2,256,128]{3,2,1,0:T(8,128)} %copy.159, f32[24,512]{1,0:T(8,128)S(1)} %bitcast.167), kind=kLoop, calls=%fused_computation.24 | loop fusion | flops 3145728 | bytes 9486336 | tf_op jit(solution)/shard_map/convert_element_type | solution.py:62
  289.5 4.9 %fusion.60 = f32[24,64,512]{2,1,0:T(8,128)} fusion(bf16[24,512,128]{2,1,0:T(8,128)(2,1)} %bitcast.142, bf16[8,24,8,128]{3,2,1,0:T(8,128)(2,1)S(1)} %get-tuple-element.9), kind=kOutput, calls=%fused_computation.65 | convolution fusion | flops 201326592 | bytes 6684672 | tf_op jit(solution)/shard_map/hrd,chd->hcr/dot_general | solution.py:81
  298.6 8.4 %multiply_reduce_fusion.4 = (f32[64,24]{0,1:T(8,128)S(1)}, f32[64,24,128]{2,0,1:T(8,128)}) fusion(f32[8,24,8,128]{3,2,1,0:T(8,128)} %get-tuple-element.8, f32[64,24]{0,1:T(8,128)S(1)} %add_rsqrt_fusion, bf16[24,512,128]{2,1,0:T(8,128)(2,1)} %fusion.16, f32[24,64,512]{2,1,0:T(8,128)} %fusion.60, f32[24,512]{1,0:T(8,128)} %copy-done.9, ...), kind=kOutput, calls=%fused_computation.60 | convolution fusion | flops 209005120 | bytes 11071488 | tf_op jit(solution)/shard_map/hcr,hrd->chd/dot_general | solution.py:89
  312.2 5.3 %fusion.15 = bf16[24,512,128]{2,1,0:T(8,128)(2,1)S(1)} fusion(f32[24,2,256,128]{3,2,1,0:T(8,128)} %copy.159, bf16[8,24,8,128]{3,2,1,0:T(8,128)(2,1)} %copy-done.5, f32[24,64,512]{2,1,0:T(8,128)} %copy-done.4, f32[24,512]{1,0:T(8,128)} %copy-done.9), kind=kOutput, calls=%fused_computation.21 | convolution fusion | flops 206831616 | bytes 13025280 | tf_op jit(solution)/shard_map/hcr,chd->hrd/dot_general | solution.py:74
  321.2 5.8 %convert_element_type.137 = bf16[1,2,256,3072]{3,2,1,0:T(8,128)(2,1)} reshape(bf16[2,256,24,128]{3,2,1,0:T(8,128)(2,1)} %copy.170) | data formatting | bytes 6291456 | tf_op jit(solution)/shard_map/convert_element_type | solution.py:167
  327.0 11.8 %multiply_reduce_fusion.2 = (f32[24,512]{1,0:T(8,128)S(1)}, f32[24,512,128]{2,1,0:T(8,128)}) fusion(f32[24,2,256,128]{3,2,1,0:T(8,128)} %copy.159, f32[24,512]{1,0:T(8,128)S(1)} %bitcast.168, f32[8,24,8,128]{3,2,1,0:T(8,128)} %get-tuple-element.8, f32[64,24]{0,1:T(8,128)S(1)} %add_rsqrt_fusion, f32[24,64,512]{2,1,0:T(8,128)} %fusion.60, ...), kind=kOutput, calls=%fused_computation.23 | convolution fusion | flops 213516352 | bytes 19814400 | tf_op jit(solution)/shard_map/hcr,chd->hrd/dot_general | solution.py:86
  338.8 8.2 %add_convert_fusion = bf16[24,512,128]{2,1,0:T(8,128)(2,1)S(1)} fusion(f32[24,512,128]{2,1,0:T(8,128)} %get-tuple-element.17, f32[24,2,256,128]{3,2,1,0:T(8,128)} %copy.159, f32[24,512]{1,0:T(8,128)S(1)} %broadcast_multiply_fusion, f32[24,512]{1,0:T(8,128)S(1)} %bitcast.169, bf16[2,256,24,128]{3,1,0,2:T(8,128)(2,1)} %copy.171), kind=kLoop, calls=%fused_computation.22 | loop fusion | flops 11010048 | bytes 18972672 | tf_op jit(solution)/shard_map/convert_element_type | solution.py:167
  350.7 5.8 %convert_element_type.143 = bf16[1,2,256,3072]{3,2,1,0:T(8,128)(2,1)} reshape(bf16[2,256,24,128]{3,2,1,0:T(8,128)(2,1)} %copy.173) | data formatting | bytes 6291456 | tf_op jit(solution)/shard_map/convert_element_type | solution.py:167
  (80 shorter events, 83.8 us)
Async XLA Ops:
  7.2 179.3 %copy-start = (bf16[2048,768]{1,0:T(8,128)(2,1)S(1)}, bf16[2048,768]{1,0:T(8,128)(2,1)}, u32[]{:S(2)}) copy-start(bf16[2048,768]{1,0:T(8,128)(2,1)} %param.9) | copy-start | bytes 9437188
  16.6 49.3 %all-to-all-start.1 = ((bf16[48,256,128]{2,1,0:T(8,128)(2,1)}), bf16[48,256,128]{2,1,0:T(8,128)(2,1)}, u32[]{:S(2)}, u32[]{:S(2)}) async-start(bf16[48,256,128]{2,1,0:T(8,128)(2,1)} %bitcast.148), calls=%async_computation.1 | async-start | bytes 6291456 | tf_op jit(solution)/shard_map/all_to_all | solution.py:134
  21.2 59.6 %all-gather.3.cloned.1.call-start = ((), (), s32[]{:S(2)}) async-start(), calls=%async_computation.6 | async-start | bytes 1638400 | tf_op jit(solution)/shard_map/all_gather | solution.py:26
  65.9 41.6 %all-to-all-start = ((bf16[48,256,128]{2,1,0:T(8,128)(2,1)}), bf16[48,256,128]{2,1,0:T(8,128)(2,1)}, u32[]{:S(2)}, u32[]{:S(2)}) async-start(bf16[48,256,128]{2,1,0:T(8,128)(2,1)} %bitcast.146), calls=%async_computation | async-start | bytes 6291456 | tf_op jit(solution)/shard_map/all_to_all | solution.py:133
  70.6 115.9 %all-gather.5.cloned.1.call-start = ((), (), s32[]{:S(2)}) async-start(), calls=%async_computation.7 | async-start | bytes 2359296 | tf_op jit(solution)/shard_map/all_gather | solution.py:118
  75.3 4.7 %copy-start.8 = (bf16[1,64,2048]{2,1,0:T(8,128)(2,1)S(1)}, bf16[1,64,2048]{2,1,0:T(8,128)(2,1)}, u32[]{:S(2)}) copy-start(bf16[1,64,2048]{2,1,0:T(8,128)(2,1)} %param.7) | copy-start | bytes 786436
  107.6 41.8 %all-to-all-start.2 = ((bf16[48,256,128]{2,1,0:T(8,128)(2,1)}), bf16[48,256,128]{2,1,0:T(8,128)(2,1)}, u32[]{:S(2)}, u32[]{:S(2)}) async-start(bf16[48,256,128]{2,1,0:T(8,128)(2,1)} %bitcast.147), calls=%async_computation.2 | async-start | bytes 6291456 | tf_op jit(solution)/shard_map/all_to_all | solution.py:135
  176.4 80.5 %all-to-all-start.3 = ((bf16[12,1024,128]{2,0,1:T(8,128)(2,1)}), bf16[12,1024,128]{2,0,1:T(8,128)(2,1)}, u32[]{:S(2)}, u32[]{:S(2)}) async-start(bf16[12,1024,128]{2,0,1:T(8,128)(2,1)} %copy.156), calls=%async_computation.3 | async-start | bytes 8388608 | tf_op jit(solution)/shard_map/all_to_all | solution.py:138
  257.0 27.1 %all-to-all-start.4 = ((bf16[8,64,768]{2,1,0:T(8,128)(2,1)}), bf16[8,64,768]{2,1,0:T(8,128)(2,1)}, u32[]{:S(2)}, u32[]{:S(2)}) async-start(bf16[8,64,768]{2,1,0:T(8,128)(2,1)} %bitcast.163), calls=%async_computation.4 | async-start | bytes 1572864 | tf_op jit(solution)/shard_map/all_to_all | solution.py:121
  263.6 92.9 %reduce-scatter.2.cloned.1.call-start = ((), (), s32[]{:S(2)}) async-start(), calls=%async_computation.8 | async-start | bytes 983040 | tf_op jit(solution)/shard_map/reduce_scatter | solution.py:178
  272.4 0.6 copy-start.6
  286.3 8.1 %copy-start.5 = (bf16[8,24,8,128]{3,2,1,0:T(8,128)(2,1)}, bf16[8,24,8,128]{3,2,1,0:T(8,128)(2,1)S(1)}, u32[]{:S(2)}) copy-start(bf16[8,24,8,128]{3,2,1,0:T(8,128)(2,1)S(1)} %get-tuple-element.9) | copy-start | bytes 1179652
  289.5 4.9 %copy-start.2 = (bf16[24,512,128]{2,1,0:T(8,128)(2,1)S(1)}, bf16[24,512,128]{2,1,0:T(8,128)(2,1)}, u32[]{:S(2)}) copy-start(bf16[24,512,128]{2,1,0:T(8,128)(2,1)} %fusion.16) | copy-start | bytes 9437188
  289.5 4.9 %copy-start.3 = (f32[8,24,8,128]{3,2,1,0:T(8,128)S(1)}, f32[8,24,8,128]{3,2,1,0:T(8,128)}, u32[]{:S(2)}) copy-start(f32[8,24,8,128]{3,2,1,0:T(8,128)} %get-tuple-element.8) | copy-start | bytes 2359300
  294.5 1.9 copy-start.1
  295.8 1.7 copy-start.4
  295.8 1.7 copy-start.9
  321.2 5.8 %copy-start.7 = (f32[2,3,8,256]{3,2,0,1:T(8,128)S(1)}, f32[2,3,8,256]{3,2,0,1:T(8,128)}, u32[]{:S(2)}) copy-start(f32[2,3,8,256]{3,2,0,1:T(8,128)} %copy-done.6) | copy-start | bytes 147460
  321.2 5.8 %copy-start.10 = (f32[24,512]{1,0:T(8,128)S(1)}, f32[24,512]{1,0:T(8,128)}, u32[]{:S(2)}) copy-start(f32[24,512]{1,0:T(8,128)} %copy-done.9) | copy-start | bytes 147460
Sparse Core Ops, SparseCore 0:
  23.6 28.4 all-gather.2
  89.1 51.7 all-gather.4
  312.3 22.0 reduce-scatter.1
where the time goes:
time: 369 us; the launch traced here: 363 us
  matrix products  89.7 us (24%)
  local copies, waits for them, and re-layouts  81 us (22%)
  blocking collectives  65.9 us (18%)
  waiting for transfers between devices  60.1 us (16%)
  other arithmetic  26.6 us (7%)
  starting transfers between devices  25.7 us (7%)
  between operations  14.2 us (4%)
    psum x1, blocking collectives, shards(): summed_kv = lax.psum(partial_kv, 'tp').astype(jnp.bfloat16)  65.9 us
    all_to_all x1, waiting for transfers between devices, shards(): lax.all_to_all(heads_first(self_key), 'tp', split_axis=0, concat_axis=1,...  34.6 us
    sub x3, matrix products, softmax_rows(): exp_terms = jnp.exp(scores - top_value)  29.3 us
    dot_general x2, matrix products, self_attention(): jnp.einsum('iqk,ikd->iqd', weights, head_value, preferred_element_type=jn...  20.4 us
    unnamed x29, local copies, waits for them, and re-layouts  20 us
    convert_element_type x4, local copies, waits for them, and re-layouts, to_rows(): return incoming_values.reshape(DENOISER_HEADS, SAMPLE_COUNT, device_rows,...  18.9 us
    all_to_all x1, waiting for transfers between devices, shards(): lax.all_to_all(heads_first(self_query), 'tp', split_axis=0, concat_axis=1...  14.6 us
    transpose x3, local copies, waits for them, and re-layouts, heads_first(): return incoming_values[0].reshape(SAMPLE_COUNT, device_rows, DENOISER_HEA...  14 us
  transfers between devices with their start and end apart: 8, of which 4 were waited for; matrix products, arithmetic and copies ran while one was open for 44% of the time, Pallas kernels for 0%

commit v1 on v0

v1 whole, which is shorter than its diff:
```python
import functools
import math

import jax
import jax.numpy as jnp
from jax import lax
from jax.experimental import pallas as pl
from jax.experimental.pallas import tpu as pltpu
from jax.sharding import PartitionSpec as P

HEAD_SIZE = 128
LLM_HEADS = 64
LLM_KV = 8
DENOISER_HEADS = 24
QUERY_TOKENS = 64
SAMPLE_COUNT = 2
PROMPT = 256
norm_eps = 1e-06
score_scale = HEAD_SIZE ** (-0.5)
NT = (((1,), (1,)), ((), ()))
TN = (((0,), (0,)), ((), ()))
NN = (((1,), (0,)), ((), ()))


def mm(a, b, dims):
    return lax.dot_general(a, b, dims, preferred_element_type=jnp.float32)


def exchange(value, mask):
    size = lax.axis_size("tp")
    return lax.ppermute(value, "tp", [(i, i ^ mask) for i in range(size)])


def tp_masks():
    size = lax.axis_size("tp")
    masks = []
    while size > 1:
        size //= 2
        masks.append(size)
    return masks


def reduce_scatter(blocks):
    masks = tp_masks()
    rest = blocks.shape[1:]
    blocks = blocks.reshape((2,) * len(masks) + rest)
    me = lax.axis_index("tp")
    for level in reversed(range(len(masks))):
        bit = (me // masks[level]) % 2
        kept = lax.dynamic_index_in_dim(blocks, bit, level, keepdims=False)
        sent = lax.dynamic_index_in_dim(blocks, 1 - bit, level, keepdims=False)
        came = exchange(sent.astype(jnp.bfloat16), masks[level])
        blocks = kept.astype(jnp.float32) + came.astype(jnp.float32)
    return blocks


def all_gather(block):
    me = lax.axis_index("tp")
    masks = tp_masks()
    rest = block.shape
    whole = block.reshape((1,) * len(masks) + rest)
    for level, mask in enumerate(masks):
        came = exchange(whole, mask)
        bit = (me // mask) % 2
        first = jnp.where(bit == 0, whole, came)
        second = jnp.where(bit == 0, came, whole)
        whole = jnp.concatenate([first, second], axis=level)
    return whole.reshape((-1,) + rest)


def llm_keys_values(llm_kv, kv_heads, first_kv_of):
    size = lax.axis_size("tp")
    me = lax.axis_index("tp")
    rows = llm_kv.shape[2]
    width = kv_heads * HEAD_SIZE
    local = llm_kv[0]
    whole = jnp.zeros((2, size, rows, width), llm_kv.dtype)
    for mask in range(size):
        other = me ^ mask
        part = lax.dynamic_slice_in_dim(local, first_kv_of(other) * HEAD_SIZE, width, 2)
        if mask:
            part = exchange(part, mask)
        whole = lax.dynamic_update_slice(whole, part[:, None], (0, other, 0, 0))
    return whole.reshape(2, size * rows, width)


def llm_hidden(llm_query, llm_kv):
    query_heads = llm_query.shape[2] // HEAD_SIZE
    group_total = LLM_HEADS // LLM_KV
    kv_heads = max(query_heads // group_total, 1)
    group_size = query_heads // kv_heads
    local_kv = llm_keys_values(llm_kv, kv_heads, lambda t: t * query_heads // group_total)
    positions = local_kv.shape[1]
    queries = llm_query[0].reshape(QUERY_TOKENS, kv_heads, group_size, HEAD_SIZE)
    keys_all = local_kv[0].reshape(positions, kv_heads, HEAD_SIZE)
    values_all = local_kv[1].reshape(positions, kv_heads, HEAD_SIZE)
    scores = (
        jnp.einsum("qkgd,pkd->kgqp", queries, keys_all, preferred_element_type=jnp.float32)
        * score_scale
    )
    allowed = jnp.arange(positions)[None, :] <= PROMPT + jnp.arange(QUERY_TOKENS)[:, None]
    scores = jnp.where(allowed, scores, -1e30)
    exp_terms = jnp.exp(scores - jnp.max(scores, axis=3, keepdims=True))
    weights = (exp_terms / jnp.sum(exp_terms, axis=3, keepdims=True)).astype(jnp.bfloat16)
    mixed_heads = jnp.einsum(
        "kgqp,pkd->qkgd", weights, values_all, preferred_element_type=jnp.float32
    )
    return mixed_heads.astype(jnp.bfloat16).reshape(QUERY_TOKENS, query_heads * HEAD_SIZE)


def context_of(llm_query, llm_kv, connector):
    hidden = llm_hidden(llm_query, llm_kv)
    every_hidden = lax.all_gather(hidden, "fsdp", axis=0, tiled=True)
    partial_kv = jnp.dot(every_hidden, connector, preferred_element_type=jnp.float32)
    size = lax.axis_size("tp")
    prompts = partial_kv.shape[0] // QUERY_TOKENS
    columns = partial_kv.shape[1]
    blocks = partial_kv.reshape(prompts, size, QUERY_TOKENS // size, columns)
    mine = reduce_scatter(blocks.transpose(1, 0, 2, 3)).astype(jnp.bfloat16)
    tokens = lax.all_to_all(mine, "fsdp", split_axis=0, concat_axis=2, tiled=True)[0]
    return all_gather(tokens).reshape(QUERY_TOKENS, -1)


def head_kernel(far, chained, *refs):
    q_ref, g_ref, ck_ref, cv_ref = refs[:4]
    refs = refs[4:]
    whole_keys, whole_values = refs[0:2], refs[2:4]
    far_refs = refs[4 : 4 + far]
    refs = refs[4 + far + (2 if chained else 0) :]
    out_ref, grad_ref, context_ref = refs
    rows = q_ref.shape[2]
    pieces = []
    for sample in range(SAMPLE_COUNT):
        query = q_ref[0, sample]
        keys = [r[0, sample] for r in whole_keys] + [r[0, sample] for r in far_refs]
        values = [r[0, sample] for r in whole_values] + [r[1, sample] for r in far_refs]
        scores = [mm(query, key, NT) for key in keys]
        top = functools.reduce(jnp.maximum, scores)
        top = jnp.max(top, axis=1, keepdims=True)
        terms = [jnp.exp((s - top) * score_scale) for s in scores]
        total = jnp.sum(functools.reduce(jnp.add, terms), axis=1, keepdims=True)
        mixed = functools.reduce(
            jnp.add, [mm(e.astype(jnp.bfloat16), v, NN) for e, v in zip(terms, values)]
        )
        pieces.append((mixed / total).astype(jnp.bfloat16))
    latent = jnp.concatenate(pieces, axis=0).astype(jnp.float32)
    inverse = lax.rsqrt(jnp.mean(latent * latent, axis=1, keepdims=True) + norm_eps)
    normed = latent * inverse
    query_round = normed.astype(jnp.bfloat16)
    key_float = ck_ref[...].astype(jnp.float32)
    key_inverse = lax.rsqrt(jnp.mean(key_float * key_float, axis=1, keepdims=True) + norm_eps)
    key_normed = key_float * key_inverse
    key_round = key_normed.astype(jnp.bfloat16)
    condition_values = cv_ref[...]
    gradient = g_ref[0].reshape(SAMPLE_COUNT * rows, HEAD_SIZE)
    exp_terms = jnp.exp(mm(key_round, query_round, NT) * score_scale)
    weights = exp_terms / jnp.sum(exp_terms, axis=0, keepdims=True)
    weights_round = weights.astype(jnp.bfloat16)
    out = latent + mm(weights_round, condition_values, TN)
    value_gradient = mm(weights_round, gradient, NN)
    weight_grad = mm(condition_values, gradient, NT)
    delta = jnp.sum(weights * weight_grad, axis=0, keepdims=True)
    score_grad = (weights * (weight_grad - delta) * score_scale).astype(jnp.bfloat16)
    query_grad = mm(score_grad, key_round, TN)
    key_grad = mm(score_grad, query_round, NN)
    grad = gradient.astype(jnp.float32) + inverse * (
        query_grad - normed * jnp.mean(query_grad * normed, axis=1, keepdims=True)
    )
    key_grad = key_inverse * (
        key_grad - key_normed * jnp.mean(key_grad * key_normed, axis=1, keepdims=True)
    )
    out_ref[0] = out.astype(jnp.bfloat16).reshape(SAMPLE_COUNT, rows, HEAD_SIZE)
    grad_ref[0] = grad.astype(jnp.bfloat16).reshape(SAMPLE_COUNT, rows, HEAD_SIZE)
    context_ref[0, 0] = key_grad.astype(jnp.bfloat16)
    context_ref[0, 1] = value_gradient.astype(jnp.bfloat16)


def attend(groups, start, taken, query, gradient, context, near, far, earlier):
    per_group = DENOISER_HEADS // groups
    rows = query.shape[2]

    def head(step):
        return step // taken * per_group + start + step % taken

    whole = pl.BlockSpec((1, SAMPLE_COUNT, rows, HEAD_SIZE), lambda i: (0, 0, 0, head(i)))
    chunk = pl.BlockSpec((2, SAMPLE_COUNT, rows, HEAD_SIZE), lambda i: (0, 0, 0, i))
    in_specs = [
        whole,
        whole,
        pl.BlockSpec((QUERY_TOKENS, HEAD_SIZE), lambda i: (0, head(i))),
        pl.BlockSpec((QUERY_TOKENS, HEAD_SIZE), lambda i: (0, DENOISER_HEADS + head(i))),
    ]
    in_specs += [whole] * len(near) + [chunk] * len(far)
    operands = [query, gradient, context, context, *near, *far]
    aliases = {}
    if earlier is not None:
        aliases = {len(operands): 0, len(operands) + 1: 1}
        operands += list(earlier)
        in_specs += [pl.BlockSpec(memory_space=pl.ANY)] * 2
    heads = groups * taken
    keys = query.shape[2] * (len(far) + 2)
    flops = heads * SAMPLE_COUNT * rows * HEAD_SIZE * (4 * keys + 12 * QUERY_TOKENS)
    return pl.pallas_call(
        functools.partial(head_kernel, len(far), earlier is not None),
        grid=(heads,),
        in_specs=in_specs,
        out_specs=[
            whole,
            whole,
            pl.BlockSpec(
                (1, 2, QUERY_TOKENS, HEAD_SIZE), lambda i: (i // taken, 0, 0, i % taken)
            ),
        ],
        out_shape=[
            jax.ShapeDtypeStruct(query.shape, jnp.bfloat16),
            jax.ShapeDtypeStruct(query.shape, jnp.bfloat16),
            jax.ShapeDtypeStruct((groups, 2, QUERY_TOKENS, taken * HEAD_SIZE), jnp.bfloat16),
        ],
        input_output_aliases=aliases,
        compiler_params=pltpu.CompilerParams(vmem_limit_bytes=40 * 1024 * 1024),
        cost_estimate=pl.CostEstimate(
            flops=4 * flops,
            bytes_accessed=heads * rows * HEAD_SIZE * 24,
            transcendentals=heads * SAMPLE_COUNT * rows * keys,
        ),
    )(*operands)


def head_pieces(per_group):
    pieces, start = [], 0
    while start < per_group:
        taken = max(1, (per_group - start) // 3)
        pieces.append((start, taken))
        start += taken
    return pieces


def shards(llm_query, llm_kv, connector, self_query, self_key, latent_value, cotangent):
    size = lax.axis_size("tp")
    groups = math.gcd(DENOISER_HEADS, size)
    masks = tp_masks()
    pieces = head_pieces(DENOISER_HEADS // groups)
    rows = self_query.shape[2]

    def piece_of(array, start, taken):
        array = array.reshape(SAMPLE_COUNT, rows, groups, -1, HEAD_SIZE)
        array = array[:, :, :, start : start + taken]
        return array.reshape(SAMPLE_COUNT, rows, groups * taken * HEAD_SIZE)

    far_parts = []
    for start, taken in pieces:
        parts = [
            jnp.stack([piece_of(self_key, start, taken), piece_of(latent_value, start, taken)])
        ]
        for mask in masks[:-1]:
            parts += [exchange(part, mask) for part in parts]
        far_parts.append(parts[1:])
    near = [
        self_key,
        exchange(self_key, masks[-1]),
        latent_value,
        exchange(latent_value, masks[-1]),
    ]
    context = context_of(llm_query, llm_kv, connector)
    earlier = None
    context_pieces = []
    for (start, taken), parts in zip(pieces, far_parts):
        far = parts + [exchange(part, masks[-1]) for part in parts]
        latent_out, self_grad, partial = attend(
            groups, start, taken, self_query, cotangent, context, near, far, earlier
        )
        earlier = (latent_out, self_grad)
        if groups == size:
            partial = reduce_scatter(partial).astype(jnp.bfloat16)
        context_pieces.append(partial)
    context_grad = jnp.concatenate(context_pieces, axis=-1)
    if groups == size:
        context_grad = context_grad[None]
    else:
        context_grad = context_grad.transpose(1, 2, 0, 3).reshape(1, 2, QUERY_TOKENS, -1)
        context_grad = lax.psum_scatter(context_grad, "tp", scatter_dimension=3, tiled=True)
    return (latent_out, self_grad, context_grad)


def solution(mesh):
    placed = (
        P("fsdp", None, "tp"),
        P("fsdp", None, "tp", None),
        P("tp", "fsdp"),
        P("fsdp", None, "tp", None),
        P("fsdp", None, "tp", None),
        P("fsdp", None, "tp", None),
        P("fsdp", None, "tp", None),
    )
    return jax.shard_map(
        shards,
        mesh=mesh,
        in_specs=placed,
        out_specs=(
            P("fsdp", None, "tp", None),
            P("fsdp", None, "tp", None),
            P("fsdp", None, None, "tp"),
        ),
        check_vma=False,
    )
```

time: 369 us -> 331 us (0.90); the launches traced: 363 us -> 329 us
  waiting for transfers between devices: 60.1 us -> 156 us
  matrix products: 89.7 us -> 8.11 us
  blocking collectives: 65.9 us -> 0 us
  Pallas kernels: 0 us -> 59.4 us
  local copies, waits for them, and re-layouts: 81 us -> 52.1 us
  other arithmetic: 26.6 us -> 17.8 us
  starting transfers between devices: 25.7 us -> 21.5 us
    ppermute x0 -> x29, waiting for transfers between devices: none -> 105 us  [exchange(): return lax.ppermute(value, 'tp', [(i, i ^ mask) for i in range(size)])]
    psum x1 -> x0, blocking collectives: 65.9 us -> none  [shards(): summed_kv = lax.psum(partial_kv, 'tp').astype(jnp.bfloat16)]
    pallas_call x0 -> x5, Pallas kernels: none -> 59.4 us  [attend(): pl.pallas_call(functools.partial(head_kernel, len(far), earlier is not No...]
    all_to_all x5 -> x1, waiting for transfers between devices: 59.3 us -> 0.01 us  [context_of(): lax.all_to_all(mine, 'fsdp', split_axis=0, concat_axis=2, tiled=True)[0]]
    dot_general x9 -> x1, matrix products: 57.4 us -> 3.37 us  [context_of(): jnp.dot(every_hidden, connector, preferred_element_type=jnp.float32)]
    all_gather x2 -> x1, waiting for transfers between devices: 0.02 us -> 50.8 us  [context_of(): every_hidden = lax.all_gather(hidden, 'fsdp', axis=0, tiled=True)]
    sub x3 -> x1, matrix products: 29.3 us -> 1.69 us  [llm_hidden(): exp_terms = jnp.exp(scores - jnp.max(scores, axis=3, keepdims=True))]
    all_to_all x5 -> x1, starting transfers between devices: 25.6 us -> 3.57 us  [context_of(): lax.all_to_all(mine, 'fsdp', split_axis=0, concat_axis=2, tiled=True)[0]]
  transfers between devices with their start and end apart: 8 -> 31, of which waited for: 4 -> 10; matrix products, arithmetic and copies ran while one was open for 44% -> 18% of each run, Pallas kernels for 0% -> 15%
where the time goes in v1:
time: 331 us; the launch traced here: 329 us
  waiting for transfers between devices  156 us (47%)
  Pallas kernels  59.4 us (18%)
  local copies, waits for them, and re-layouts  52.1 us (16%)
  starting transfers between devices  21.5 us (6%)
  other arithmetic  17.8 us (5%)
  between operations  14.5 us (4%)
  matrix products  8.11 us (2%)
    ppermute x29, waiting for transfers between devices, exchange(): return lax.ppermute(value, 'tp', [(i, i ^ mask) for i in range(size)])  105 us
    pallas_call x5, Pallas kernels, attend(): pl.pallas_call(functools.partial(head_kernel, len(far), earlier is not No...  59.4 us
    all_gather x1, waiting for transfers between devices, context_of(): every_hidden = lax.all_gather(hidden, 'fsdp', axis=0, tiled=True)  50.8 us
    another operation x10, local copies, waits for them, and re-layouts, shards(): jnp.stack([piece_of(self_key, start, taken), piece_of(latent_value, start...  21 us
    ppermute x29, starting transfers between devices, exchange(): return lax.ppermute(value, 'tp', [(i, i ^ mask) for i in range(size)])  17.9 us
    unnamed x30, local copies, waits for them, and re-layouts  15.1 us
    another operation x5, other arithmetic, shards(): jnp.stack([piece_of(self_key, start, taken), piece_of(latent_value, start...  11 us
    slice x4, local copies, waits for them, and re-layouts, piece_of(): array = array[:, :, :, start:start + taken]  10.5 us
  transfers between devices with their start and end apart: 31, of which 10 were waited for; matrix products, arithmetic and copies ran while one was open for 18% of the time, Pallas kernels for 15%

profile of v1, /device:TPU:0, one launch (start us, length us, event | category | flops | bytes accessed | tf_op | source)
XLA Modules:
  0.0 329.4 jit_solution(16696809305210461000)
XLA Ops:
  9.5 2.5 collective-permute-start.1
  19.8 3.0 fusion.3
  23.8 50.8 %all-gather.2.cloned.1.call-done = bf16[512,2048]{1,0:T(8,128)(2,1)} async-done(((bf16[64,2048]{1,0:T(8,128)(2,1)}), bf16[512,2048]{1,0:T(8,128)(2,1)}) %all-gather.2.cloned.1.call-update) | async-done | bytes 2097168 | tf_op jit(solution)/shard_map/all_gather | solution.py:113
  74.7 3.4 %fusion.56 = f32[512,768]{1,0:T(8,128)S(1)} fusion(bf16[512,2048]{1,0:T(8,128)(2,1)} %all-gather.2.cloned.1.call-done, bf16[2048,768]{1,0:T(8,128)(2,1)S(1)} %copy-done), kind=kOutput, calls=%fused_computation.82 | convolution fusion | flops 1610612736 | bytes 6815744 | tf_op jit(solution)/shard_map/dot_general | solution.py:114
  86.1 2.8 copy.84
  88.8 4.6 %copy.86 = bf16[1,2,256,3072]{2,3,1,0:T(8,128)(2,1)} copy(bf16[1,2,256,3072]{3,2,1,0:T(8,128)(2,1)} %refs_6_.9) | data formatting | bytes 6291456 | tf_op args[5]
  93.5 2.4 slice.60
  98.1 2.3 slice.61
  100.4 2.3 copy.116
  102.7 3.1 pad_maximum_fusion
  108.0 3.6 %all-to-all-start = ((bf16[8,16,768]{2,1,0:T(8,128)(2,1)}), bf16[8,16,768]{2,1,0:T(8,128)(2,1)S(1)}, u32[]{:S(2)}, u32[]{:S(2)}) async-start(bf16[8,16,768]{2,1,0:T(8,128)(2,1)} %fusion.5), calls=%async_computation | async-start | bytes 393216 | tf_op jit(solution)/shard_map/all_to_all | solution.py:120
  111.6 2.9 fusion.48
  116.6 2.9 fusion.49
  132.5 26.2 %collective-permute-done.5 = bf16[1,1,16,6144]{3,2,1,0:T(8,128)(2,1)S(1)} collective-permute-done((bf16[1,1,16,6144]{3,2,1,0:T(8,128)(2,1)S(1)}, bf16[1,1,16,6144]{3,2,1,0:T(8,128)(2,1)S(1)}, u32[]{:S(2)}, u32[]{:S(2)}) %collective-permute-start.5) | collective-permute-done | bytes 196640 | tf_op jit(solution)/shard_map/ppermute | solution.py:31
  161.7 19.5 %collective-permute-done.15.refs_8_ = bf16[2,2,256,512]{3,2,1,0:T(8,128)(2,1)} collective-permute-done((bf16[2,2,256,512]{3,2,1,0:T(8,128)(2,1)}, bf16[2,2,256,512]{3,2,1,0:T(8,128)(2,1)}, u32[]{:S(2)}, u32[]{:S(2)}) %collective-permute-start.15) | collective-permute-done | bytes 1048608 | tf_op jit(solution)/shard_map/ppermute | solution.py:31
  189.5 2.4 pad_maximum_fusion.2
  193.4 9.3 %collective-permute-done.13.refs_8_ = bf16[2,2,256,512]{3,2,1,0:T(8,128)(2,1)} collective-permute-done((bf16[2,2,256,512]{3,2,1,0:T(8,128)(2,1)}, bf16[2,2,256,512]{3,2,1,0:T(8,128)(2,1)}, u32[]{:S(2)}, u32[]{:S(2)}) %collective-permute-start.13) | collective-permute-done | bytes 1048608 | tf_op jit(solution)/shard_map/ppermute | solution.py:31
  205.8 23.2 %collective-permute-done.11.refs_8_ = bf16[2,2,256,512]{3,2,1,0:T(8,128)(2,1)S(1)} collective-permute-done((bf16[2,2,256,512]{3,2,1,0:T(8,128)(2,1)}, bf16[2,2,256,512]{3,2,1,0:T(8,128)(2,1)S(1)}, u32[]{:S(2)}, u32[]{:S(2)}) %collective-permute-start.11) | collective-permute-done | bytes 1048608 | tf_op jit(solution)/shard_map/ppermute | solution.py:31
  229.1 20.5 %collective-permute-done.9.refs_8_ = bf16[2,2,256,512]{3,2,1,0:T(8,128)(2,1)S(1)} collective-permute-done((bf16[2,2,256,512]{3,2,1,0:T(8,128)(2,1)}, bf16[2,2,256,512]{3,2,1,0:T(8,128)(2,1)S(1)}, u32[]{:S(2)}, u32[]{:S(2)}) %collective-permute-start.9) | collective-permute-done | bytes 1048608 | tf_op jit(solution)/shard_map/ppermute | solution.py:31
  252.1 18.6 %shard_map.94 = (bf16[1,2,256,3072]{3,2,1,0:T(8,128)(2,1)}, bf16[1,2,256,3072]{3,2,1,0:T(8,128)(2,1)}, bf16[4,2,64,256]{3,2,1,0:T(8,128)(2,1)S(1)}) custom-call(bf16[1,2,256,3072]{3,2,1,0:T(8,128)(2,1)S(1)} %copy-done.4, bf16[1,2,256,3072]{3,2,1,0:T(8,128)(2,1)S(1)} %copy-done.5, bf16[64,6144]{1,0:T(8,128)(2,1)S(1)} %bitcast.158, ...), custom_call_target="tpu_custom_call" | custom-call | flops 10200547328 | bytes 6291456 | tf_op jit(solution)/shard_map/pallas_call | solution.py:203
  270.8 10.1 %shard_map.95 = (bf16[1,2,256,3072]{3,2,1,0:T(8,128)(2,1)}, bf16[1,2,256,3072]{3,2,1,0:T(8,128)(2,1)}, bf16[4,2,64,128]{3,2,1,0:T(8,128)(2,1)S(1)}) custom-call(bf16[1,2,256,3072]{3,2,1,0:T(8,128)(2,1)S(1)} %copy-done.4, bf16[1,2,256,3072]{3,2,1,0:T(8,128)(2,1)S(1)} %copy-done.5, ...), custom_call_target="tpu_custom_call", output_to_operand_aliasing={{0}: (10, {}), {1}: (11, {})} | custom-call | flops 5100273664 | bytes 3145728 | tf_op jit(solution)/shard_map/pallas_call | solution.py:203
  280.9 10.1 %shard_map.96 = (bf16[1,2,256,3072]{3,2,1,0:T(8,128)(2,1)}, bf16[1,2,256,3072]{3,2,1,0:T(8,128)(2,1)}, bf16[4,2,64,128]{3,2,1,0:T(8,128)(2,1)S(1)}) custom-call(bf16[1,2,256,3072]{3,2,1,0:T(8,128)(2,1)S(1)} %copy-done.4, bf16[1,2,256,3072]{3,2,1,0:T(8,128)(2,1)S(1)} %copy-done.5, ...), custom_call_target="tpu_custom_call", output_to_operand_aliasing={{0}: (10, {}), {1}: (11, {})} | custom-call | flops 5100273664 | bytes 3145728 | tf_op jit(solution)/shard_map/pallas_call | solution.py:203
  291.0 10.1 %shard_map.97 = (bf16[1,2,256,3072]{3,2,1,0:T(8,128)(2,1)}, bf16[1,2,256,3072]{3,2,1,0:T(8,128)(2,1)}, bf16[4,2,64,128]{3,2,1,0:T(8,128)(2,1)S(1)}) custom-call(bf16[1,2,256,3072]{3,2,1,0:T(8,128)(2,1)S(1)} %copy-done.4, bf16[1,2,256,3072]{3,2,1,0:T(8,128)(2,1)S(1)} %copy-done.5, ...), custom_call_target="tpu_custom_call", output_to_operand_aliasing={{0}: (10, {}), {1}: (11, {})} | custom-call | flops 5100273664 | bytes 3145728 | tf_op jit(solution)/shard_map/pallas_call | solution.py:203
  301.1 10.5 %shard_map.98 = (bf16[1,2,256,3072]{3,2,1,0:T(8,128)(2,1)}, bf16[1,2,256,3072]{3,2,1,0:T(8,128)(2,1)}, bf16[4,2,64,128]{3,2,1,0:T(8,128)(2,1)S(1)}) custom-call(bf16[1,2,256,3072]{3,2,1,0:T(8,128)(2,1)S(1)} %copy-done.4, bf16[1,2,256,3072]{3,2,1,0:T(8,128)(2,1)S(1)} %copy-done.5, ...), custom_call_target="tpu_custom_call", output_to_operand_aliasing={{0}: (10, {}), {1}: (11, {})} | custom-call | flops 5100273664 | bytes 3145728 | tf_op jit(solution)/shard_map/pallas_call | solution.py:203
  (139 shorter events, 67.8 us)
Async XLA Ops:
  7.2 67.5 %all-gather.2.cloned.1.call-start = ((), (), s32[]{:S(2)}) async-start(), calls=%async_computation.1 | async-start | bytes 2359296 | tf_op jit(solution)/shard_map/all_gather | solution.py:113
  9.1 6.4 %collective-permute-start = (bf16[2,80,256]{2,1,0:T(8,128)(2,1)}, bf16[2,80,256]{2,1,0:T(8,128)(2,1)S(1)}, u32[]{:S(2)}, u32[]{:S(2)}) collective-permute-start(bf16[2,80,256]{2,1,0:T(8,128)(2,1)} %get-tuple-element.48), channel_id=1, source_target_pairs={{0,1},{1,0},{2,3},{3,2},{4,5},{5,4},{6,7},{7,6},{8,9},{9,8},{10,11... | collective-permute-start | bytes 245768 | tf_op jit(solution)/shard_map/ppermute | solution.py:31
  9.5 6.0 %collective-permute-start.1 = (bf16[2,80,256]{2,1,0:T(8,128)(2,1)S(1)}, bf16[2,80,256]{2,1,0:T(8,128)(2,1)S(1)}, u32[]{:S(2)}, u32[]{:S(2)}) collective-permute-start(bf16[2,80,256]{2,1,0:T(8,128)(2,1)S(1)} %get-tuple-element.49), channel_id=1, source_target_pairs={{0,2},{1,3},{2,0},{3,1},{4,6},{5,7},{6,4},{7,5},{8,10},{9,11},{10,... | collective-permute-start | bytes 245768 | tf_op jit(solution)/shard_map/ppermute | solution.py:31
  12.0 4.6 %collective-permute-start.2 = (bf16[2,80,256]{2,1,0:T(8,128)(2,1)S(1)}, bf16[2,80,256]{2,1,0:T(8,128)(2,1)S(1)}, u32[]{:S(2)}, u32[]{:S(2)}) collective-permute-start(bf16[2,80,256]{2,1,0:T(8,128)(2,1)S(1)} %get-tuple-element.47), channel_id=1, source_target_pairs={{0,3},{1,2},{2,1},{3,0},{4,7},{5,6},{6,5},{7,4},{8,11},{9,10},{10,... | collective-permute-start | bytes 245768 | tf_op jit(solution)/shard_map/ppermute | solution.py:31
  84.1 22.2 %collective-permute-start.4 = (bf16[8,16,768]{2,1,0:T(8,128)(2,1)S(1)}, bf16[8,16,768]{2,1,0:T(8,128)(2,1)S(1)}, u32[]{:S(2)}, u32[]{:S(2)}) collective-permute-start(bf16[8,16,768]{2,1,0:T(8,128)(2,1)S(1)} %fusion.7), channel_id=1, source_target_pairs={{0,2},{1,3},{2,0},{3,1},{4,6},{5,7},{6,4},{7,5},{8,10},{9,11},{10,... | collective-permute-start | bytes 589832 | tf_op jit(solution)/shard_map/ppermute | solution.py:31
  85.6 164.1 %collective-permute-start.7 = (bf16[1,2,256,3072]{3,2,1,0:T(8,128)(2,1)S(1)}, bf16[1,2,256,3072]{3,2,1,0:T(8,128)(2,1)}, u32[]{:S(2)}, u32[]{:S(2)}) collective-permute-start(bf16[1,2,256,3072]{3,2,1,0:T(8,128)(2,1)S(1)} %copy-done.2), channel_id=1, source_target_pairs={{0,1},{1,0},{2,3},{3,2},{4,5},{5,4},{6,7},{7,6},{8,9},{9,8},{10,11... | collective-permute-start | bytes 9437192 | tf_op jit(solution)/shard_map/ppermute | solution.py:31
  85.6 164.6 %collective-permute-start.8 = (bf16[1,2,256,3072]{3,2,1,0:T(8,128)(2,1)}, bf16[1,2,256,3072]{3,2,1,0:T(8,128)(2,1)}, u32[]{:S(2)}, u32[]{:S(2)}) collective-permute-start(bf16[1,2,256,3072]{3,2,1,0:T(8,128)(2,1)} %refs_6_.9), channel_id=1, source_target_pairs={{0,1},{1,0},{2,3},{3,2},{4,5},{5,4},{6,7},{7,6},{8,9},{9,8},{10,11... | collective-permute-start | bytes 9437192 | tf_op jit(solution)/shard_map/ppermute | solution.py:31
  105.7 86.1 %collective-permute-start.17 = (bf16[2,2,256,1024]{3,2,1,0:T(8,128)(2,1)}, bf16[2,2,256,1024]{3,2,1,0:T(8,128)(2,1)}, u32[]{:S(2)}, u32[]{:S(2)}) collective-permute-start(bf16[2,2,256,1024]{3,2,1,0:T(8,128)(2,1)} %pad_maximum_fusion), channel_id=1, source_target_pairs={{0,2},{1,3},{2,0},{3,1},{4,6},{5,7},{6,4},{7,5},{8,10},{9,11},{10,... | collective-permute-start | bytes 6291464 | tf_op jit(solution)/shard_map/ppermute | solution.py:31
  108.0 13.5 %all-to-all-start = ((bf16[8,16,768]{2,1,0:T(8,128)(2,1)}), bf16[8,16,768]{2,1,0:T(8,128)(2,1)S(1)}, u32[]{:S(2)}, u32[]{:S(2)}) async-start(bf16[8,16,768]{2,1,0:T(8,128)(2,1)} %fusion.5), calls=%async_computation | async-start | bytes 393216 | tf_op jit(solution)/shard_map/all_to_all | solution.py:120
  121.7 36.9 %collective-permute-start.5 = (bf16[1,1,16,6144]{3,2,1,0:T(8,128)(2,1)S(1)}, bf16[1,1,16,6144]{3,2,1,0:T(8,128)(2,1)S(1)}, u32[]{:S(2)}, u32[]{:S(2)}) collective-permute-start(bf16[1,1,16,6144]{3,2,1,0:T(8,128)(2,1)S(1)} %reshape_squeeze.15), channel_id=1, source_target_pairs={{0,2},{1,3},{2,0},{3,1},{4,6},{5,7},{6,4},{7,5},{8,10},{9,11},{10,... | collective-permute-start | bytes 589832 | tf_op jit(solution)/shard_map/ppermute | solution.py:31
  125.5 55.7 %collective-permute-start.15 = (bf16[2,2,256,512]{3,2,1,0:T(8,128)(2,1)}, bf16[2,2,256,512]{3,2,1,0:T(8,128)(2,1)}, u32[]{:S(2)}, u32[]{:S(2)}) collective-permute-start(bf16[2,2,256,512]{3,2,1,0:T(8,128)(2,1)} %pad_maximum_fusion.4), channel_id=1, source_target_pairs={{0,2},{1,3},{2,0},{3,1},{4,6},{5,7},{6,4},{7,5},{8,10},{9,11},{10,... | collective-permute-start | bytes 3145736 | tf_op jit(solution)/shard_map/ppermute | solution.py:31
  159.3 43.4 %collective-permute-start.13 = (bf16[2,2,256,512]{3,2,1,0:T(8,128)(2,1)}, bf16[2,2,256,512]{3,2,1,0:T(8,128)(2,1)}, u32[]{:S(2)}, u32[]{:S(2)}) collective-permute-start(bf16[2,2,256,512]{3,2,1,0:T(8,128)(2,1)} %pad_maximum_fusion.3), channel_id=1, source_target_pairs={{0,2},{1,3},{2,0},{3,1},{4,6},{5,7},{6,4},{7,5},{8,10},{9,11},{10,... | collective-permute-start | bytes 3145736 | tf_op jit(solution)/shard_map/ppermute | solution.py:31
  181.2 22.1 %collective-permute-start.6 = (bf16[2,1,16,6144]{3,2,1,0:T(8,128)(2,1)}, bf16[2,1,16,6144]{3,2,1,0:T(8,128)(2,1)}, u32[]{:S(2)}, u32[]{:S(2)}) collective-permute-start(bf16[2,1,16,6144]{3,2,1,0:T(8,128)(2,1)} %pad_maximum_fusion.6), channel_id=1, source_target_pairs={{0,1},{1,0},{2,3},{3,2},{4,5},{5,4},{6,7},{7,6},{8,9},{9,8},{10,11... | collective-permute-start | bytes 1179656 | tf_op jit(solution)/shard_map/ppermute | solution.py:31
  191.8 58.4 %collective-permute-start.18 = (bf16[2,2,256,1024]{3,2,1,0:T(8,128)(2,1)}, bf16[2,2,256,1024]{3,2,1,0:T(8,128)(2,1)}, u32[]{:S(2)}, u32[]{:S(2)}) collective-permute-start(bf16[2,2,256,1024]{3,2,1,0:T(8,128)(2,1)} %collective-permute-done.17.refs_8_), channel_id=1, source_target_pairs={{0,1},{1,0},{2,3},{3,2},{4,5},{5,4},{6,7},{7,6},{8,9},{9,8},{10,11... | collective-permute-start | bytes 6291464 | tf_op jit(solution)/shard_map/ppermute | solution.py:31
  202.8 26.3 %collective-permute-start.11 = (bf16[2,2,256,512]{3,2,1,0:T(8,128)(2,1)}, bf16[2,2,256,512]{3,2,1,0:T(8,128)(2,1)S(1)}, u32[]{:S(2)}, u32[]{:S(2)}) collective-permute-start(bf16[2,2,256,512]{3,2,1,0:T(8,128)(2,1)} %pad_maximum_fusion.2), channel_id=1, source_target_pairs={{0,2},{1,3},{2,0},{3,1},{4,6},{5,7},{6,4},{7,5},{8,10},{9,11},{10,... | collective-permute-start | bytes 3145736 | tf_op jit(solution)/shard_map/ppermute | solution.py:31
  203.3 46.3 %collective-permute-start.9 = (bf16[2,2,256,512]{3,2,1,0:T(8,128)(2,1)}, bf16[2,2,256,512]{3,2,1,0:T(8,128)(2,1)S(1)}, u32[]{:S(2)}, u32[]{:S(2)}) collective-permute-start(bf16[2,2,256,512]{3,2,1,0:T(8,128)(2,1)} %pad_maximum_fusion.1), channel_id=1, source_target_pairs={{0,2},{1,3},{2,0},{3,1},{4,6},{5,7},{6,4},{7,5},{8,10},{9,11},{10,... | collective-permute-start | bytes 3145736 | tf_op jit(solution)/shard_map/ppermute | solution.py:31
  229.1 41.7 %collective-permute-start.16 = (bf16[2,2,256,512]{3,2,1,0:T(8,128)(2,1)}, bf16[2,2,256,512]{3,2,1,0:T(8,128)(2,1)}, u32[]{:S(2)}, u32[]{:S(2)}) collective-permute-start(bf16[2,2,256,512]{3,2,1,0:T(8,128)(2,1)} %collective-permute-done.15.refs_8_), channel_id=1, source_target_pairs={{0,1},{1,0},{2,3},{3,2},{4,5},{5,4},{6,7},{7,6},{8,9},{9,8},{10,11... | collective-permute-start | bytes 3145736 | tf_op jit(solution)/shard_map/ppermute | solution.py:31
  249.6 31.3 %collective-permute-start.14 = (bf16[2,2,256,512]{3,2,1,0:T(8,128)(2,1)}, bf16[2,2,256,512]{3,2,1,0:T(8,128)(2,1)}, u32[]{:S(2)}, u32[]{:S(2)}) collective-permute-start(bf16[2,2,256,512]{3,2,1,0:T(8,128)(2,1)} %collective-permute-done.13.refs_8_), channel_id=1, source_target_pairs={{0,1},{1,0},{2,3},{3,2},{4,5},{5,4},{6,7},{7,6},{8,9},{9,8},{10,11... | collective-permute-start | bytes 3145736 | tf_op jit(solution)/shard_map/ppermute | solution.py:31
  249.7 41.4 %collective-permute-start.12 = (bf16[2,2,256,512]{3,2,1,0:T(8,128)(2,1)S(1)}, bf16[2,2,256,512]{3,2,1,0:T(8,128)(2,1)S(1)}, u32[]{:S(2)}, u32[]{:S(2)}) collective-permute-start(bf16[2,2,256,512]{3,2,1,0:T(8,128)(2,1)S(1)} %collective-permute-done.11.refs_8_), channel_id=1, source_target_pairs={{0,1},{1,0},{2,3},{3,2},{4,5},{5,4},{6,7},{7,6},{8,9},{9,8},{10,11... | collective-permute-start | bytes 3145736 | tf_op jit(solution)/shard_map/ppermute | solution.py:31
  250.2 50.9 %collective-permute-start.10 = (bf16[2,2,256,512]{3,2,1,0:T(8,128)(2,1)S(1)}, bf16[2,2,256,512]{3,2,1,0:T(8,128)(2,1)S(1)}, u32[]{:S(2)}, u32[]{:S(2)}) collective-permute-start(bf16[2,2,256,512]{3,2,1,0:T(8,128)(2,1)S(1)} %collective-permute-done.9.refs_8_), channel_id=1, source_target_pairs={{0,1},{1,0},{2,3},{3,2},{4,5},{5,4},{6,7},{7,6},{8,9},{9,8},{10,11... | collective-permute-start | bytes 3145736 | tf_op jit(solution)/shard_map/ppermute | solution.py:31
  313.3 8.5 %collective-permute-start.28 = (bf16[2,64,128]{2,1,0:T(8,128)(2,1)S(1)}, bf16[2,64,128]{2,1,0:T(8,128)(2,1)S(1)}, u32[]{:S(2)}, u32[]{:S(2)}) collective-permute-start(bf16[2,64,128]{2,1,0:T(8,128)(2,1)S(1)} %fusion.24), channel_id=1, source_target_pairs={{0,2},{1,3},{2,0},{3,1},{4,6},{5,7},{6,4},{7,5},{8,10},{9,11},{10,... | collective-permute-start | bytes 98312 | tf_op jit(solution)/shard_map/ppermute | solution.py:31
  314.0 7.8 %collective-permute-start.26 = (bf16[2,64,128]{2,1,0:T(8,128)(2,1)S(1)}, bf16[2,64,128]{2,1,0:T(8,128)(2,1)S(1)}, u32[]{:S(2)}, u32[]{:S(2)}) collective-permute-start(bf16[2,64,128]{2,1,0:T(8,128)(2,1)S(1)} %fusion.23), channel_id=1, source_target_pairs={{0,2},{1,3},{2,0},{3,1},{4,6},{5,7},{6,4},{7,5},{8,10},{9,11},{10,... | collective-permute-start | bytes 98312 | tf_op jit(solution)/shard_map/ppermute | solution.py:31
  315.5 6.2 %collective-permute-start.24 = (bf16[2,64,128]{2,1,0:T(8,128)(2,1)S(1)}, bf16[2,64,128]{2,1,0:T(8,128)(2,1)S(1)}, u32[]{:S(2)}, u32[]{:S(2)}) collective-permute-start(bf16[2,64,128]{2,1,0:T(8,128)(2,1)S(1)} %fusion.22), channel_id=1, source_target_pairs={{0,2},{1,3},{2,0},{3,1},{4,6},{5,7},{6,4},{7,5},{8,10},{9,11},{10,... | collective-permute-start | bytes 98312 | tf_op jit(solution)/shard_map/ppermute | solution.py:31
  316.3 4.3 %collective-permute-start.20 = (bf16[2,64,256]{2,1,0:T(8,128)(2,1)S(1)}, bf16[2,64,256]{2,1,0:T(8,128)(2,1)S(1)}, u32[]{:S(2)}, u32[]{:S(2)}) collective-permute-start(bf16[2,64,256]{2,1,0:T(8,128)(2,1)S(1)} %fusion.15), channel_id=1, source_target_pairs={{0,2},{1,3},{2,0},{3,1},{4,6},{5,7},{6,4},{7,5},{8,10},{9,11},{10,... | collective-permute-start | bytes 196616 | tf_op jit(solution)/shard_map/ppermute | solution.py:31
  (20 other events, 210.8 us)
Sparse Core Ops, SparseCore 0:
  23.9 50.6 all-gather.1

commit v2 on v1

--- a/solution.py
+++ b/solution.py
@@ -235,7 +235,569 @@
     return pieces
 
 
+MESH = pl.DeviceIdType.MESH
+DEPTH = 3
+
+
+def self_head(query_of, keys_of, values_of):
+    pieces = []
+    for sample in range(SAMPLE_COUNT):
+        scores = [mm(query_of(sample), key, NT) for key in keys_of(sample)]
+        top = jnp.max(functools.reduce(jnp.maximum, scores), axis=1, keepdims=True)
+        terms = [jnp.exp((s - top) * score_scale) for s in scores]
+        total = jnp.sum(functools.reduce(jnp.add, terms), axis=1, keepdims=True)
+        mixed = functools.reduce(
+            jnp.add, [mm(e.astype(jnp.bfloat16), v, NN) for e, v in zip(terms, values_of(sample))]
+        )
+        pieces.append((mixed / total).astype(jnp.bfloat16))
+    return pieces
+
+
+def cross_head(latent, context_keys, condition_values, gradient):
+    latent = latent.astype(jnp.float32)
+    inverse = lax.rsqrt(jnp.mean(latent * latent, axis=1, keepdims=True) + norm_eps)
+    normed = latent * inverse
+    query_round = normed.astype(jnp.bfloat16)
+    key_float = context_keys.astype(jnp.float32)
+    key_inverse = lax.rsqrt(jnp.mean(key_float * key_float, axis=1, keepdims=True) + norm_eps)
+    key_normed = key_float * key_inverse
+    key_round = key_normed.astype(jnp.bfloat16)
+    exp_terms = jnp.exp(mm(key_round, query_round, NT) * score_scale)
+    weights = exp_terms / jnp.sum(exp_terms, axis=0, keepdims=True)
+    weights_round = weights.astype(jnp.bfloat16)
+    out = latent + mm(weights_round, condition_values, TN)
+    value_gradient = mm(weights_round, gradient, NN)
+    weight_grad = mm(condition_values, gradient, NT)
+    delta = jnp.sum(weights * weight_grad, axis=0, keepdims=True)
+    score_grad = (weights * (weight_grad - delta) * score_scale).astype(jnp.bfloat16)
+    query_grad = mm(score_grad, key_round, TN)
+    key_grad = mm(score_grad, query_round, NN)
+    grad = gradient.astype(jnp.float32) + inverse * (
+        query_grad - normed * jnp.mean(query_grad * normed, axis=1, keepdims=True)
+    )
+    key_grad = key_inverse * (
+        key_grad - key_normed * jnp.mean(key_grad * key_normed, axis=1, keepdims=True)
+    )
+    return tuple(a.astype(jnp.bfloat16) for a in (out, grad, key_grad, value_gradient))
+
+
+def whole_kernel(
+    size,
+    prompts,
+    llm_query_ref,
+    llm_kv_ref,
+    connector_ref,
+    query_ref,
+    key_ref,
+    value_ref,
+    cotangent_ref,
+    out_ref,
+    grad_ref,
+    context_grad_ref,
+    kv,
+    q_all,
+    g_all,
+    latent,
+    llm_q,
+    llm_parts,
+    connector,
+    hidden,
+    partial,
+    sum_out,
+    sum_in,
+    half,
+    half_out,
+    half_in,
+    mine,
+    context,
+    pg,
+    pg_near,
+    pg_out,
+    pg_far,
+    load_sem,
+    whole_sem,
+    far_send,
+    far_recv,
+    near_send,
+    near_recv,
+    pass_send,
+    pass_recv,
+    llm_send,
+    llm_recv,
+    hidden_send,
+    hidden_recv,
+    sum_send,
+    sum_recv,
+    token_send,
+    token_recv,
+    gather_send,
+    gather_recv,
+    pg_send,
+    pg_recv,
+    out_sem,
+):
+    me = lax.axis_index("tp")
+    row = lax.axis_index("fsdp")
+    core = me % 2
+    half_index = me // 2
+    near = me + 1 - 2 * core
+    far = me + 2 - 4 * half_index
+    heads = DENOISER_HEADS
+    per = heads // size
+    rows = query_ref.shape[2]
+    block = QUERY_TOKENS // size
+    llm_width = llm_parts.shape[3]
+    columns = connector_ref.shape[1]
+    bf = jnp.bfloat16
+
+    def peer_at(distance):
+        low, high = distance % 2, distance // 2
+        new_core = core + low - 2 * core * low
+        new_half = half_index + high - 2 * half_index * high
+        return new_half * 2 + new_core
+
+    def remote(src, dst, send, recv, **where):
+        return pltpu.make_async_remote_copy(
+            src_ref=src,
+            dst_ref=dst,
+            send_sem=send,
+            recv_sem=recv,
+            device_id=where,
+            device_id_type=MESH,
+        )
+
+    def head_of(i):
+        return (i % size) * per + i // size
+
+    def cols(i):
+        return pl.ds(pl.multiple_of(head_of(i) * HEAD_SIZE, HEAD_SIZE), HEAD_SIZE)
+
+    def load(i, which):
+        source = (key_ref, value_ref)[which]
+        return pltpu.make_async_copy(
+            source.at[0, :, :, cols(i)], kv.at[0, i, which], load_sem.at[i, which]
+        )
+
+    def far_copy(i):
+        return remote(kv.at[0, i], kv.at[2, i], far_send.at[i], far_recv.at[i], tp=far)
+
+    def near_copy(i):
+        return remote(kv.at[0, i], kv.at[1, i], near_send.at[i], near_recv.at[i], tp=near)
+
+    def pass_copy(i):
+        return remote(kv.at[2, i], kv.at[3, i], pass_send.at[i], pass_recv.at[i], tp=near)
+
+    def llm_copy(d):
+        start = pl.multiple_of(peer_at(d) * llm_width, HEAD_SIZE)
+        return remote(
+            llm_kv_ref.at[0, :, :, pl.ds(start, llm_width)],
+            llm_parts.at[me],
+            llm_send.at[d - 1],
+            llm_recv.at[d - 1],
+            tp=peer_at(d),
+        )
+
+    def llm_came(d):
+        there = llm_parts.at[peer_at(d)]
+        return remote(there, there, llm_send.at[d - 1], llm_recv.at[d - 1], tp=peer_at(d))
+
+    own_start = pl.multiple_of(me * llm_width, HEAD_SIZE)
+    llm_q_load = pltpu.make_async_copy(llm_query_ref.at[0], llm_q, whole_sem.at[0])
+    llm_own_load = pltpu.make_async_copy(
+        llm_kv_ref.at[0, :, :, pl.ds(own_start, llm_width)], llm_parts.at[me], whole_sem.at[1]
+    )
+    q_load = pltpu.make_async_copy(query_ref.at[0], q_all, whole_sem.at[2])
+    g_load = pltpu.make_async_copy(cotangent_ref.at[0], g_all, whole_sem.at[3])
+    connector_load = pltpu.make_async_copy(connector_ref, connector, whole_sem.at[4])
+
+    llm_q_load.start()
+    llm_own_load.start()
+
+    @pl.loop(0, heads)
+    def _(i):
+        load(i, 0).start()
+        load(i, 1).start()
+
+    q_load.start()
+    connector_load.start()
+    g_load.start()
+
+    barrier = pltpu.get_barrier_semaphore()
+    for d in range(1, size):
+        pl.semaphore_signal(barrier, inc=1, device_id={"tp": peer_at(d)}, device_id_type=MESH)
+    for d in range(1, prompts):
+        pl.semaphore_signal(
+            barrier, inc=1, device_id={"fsdp": (row + d) % prompts}, device_id_type=MESH
+        )
+    pl.semaphore_wait(barrier, size - 1 + prompts - 1)
+
+    for d in range(size - 1, 0, -1):
+        llm_copy(d).start()
+
+    @pl.loop(0, DEPTH)
+    def _(i):
+        load(i, 0).wait()
+        load(i, 1).wait()
+        far_copy(i).start()
+        near_copy(i).start()
+
+    @pl.loop(DEPTH, heads)
+    def _(i):
+        load(i, 0).wait()
+        load(i, 1).wait()
+        near_copy(i).start()
+
+    llm_q_load.wait()
+    llm_own_load.wait()
+    for d in range(1, size):
+        llm_came(d).wait_recv()
+    kv_heads = llm_width // HEAD_SIZE
+    group = llm_q.shape[1] // llm_width
+    positions = size * llm_parts.shape[2]
+    shape = (group * QUERY_TOKENS, positions)
+    token = lax.broadcasted_iota(jnp.int32, shape, 0) % QUERY_TOKENS
+    allowed = lax.broadcasted_iota(jnp.int32, shape, 1) <= PROMPT + token
+    for k in range(kv_heads):
+        at = slice(k * HEAD_SIZE, (k + 1) * HEAD_SIZE)
+        base = k * group * HEAD_SIZE
+        stacked = jnp.concatenate(
+            [llm_q[:, base + j * HEAD_SIZE : base + (j + 1) * HEAD_SIZE] for j in range(group)], 0
+        )
+        keys = jnp.concatenate([llm_parts[j, 0, :, at] for j in range(size)], 0)
+        values = jnp.concatenate([llm_parts[j, 1, :, at] for j in range(size)], 0)
+        scores = jnp.where(allowed, mm(stacked, keys, NT) * score_scale, -1e30)
+        terms = jnp.exp(scores - jnp.max(scores, axis=1, keepdims=True))
+        total = jnp.sum(terms, axis=1, keepdims=True)
+        mixed = (mm((terms / total).astype(bf), values, NN)).astype(bf)
+        for j in range(group):
+            hidden[row, :, base + j * HEAD_SIZE : base + (j + 1) * HEAD_SIZE] = mixed[
+                j * QUERY_TOKENS : (j + 1) * QUERY_TOKENS
+            ]
+
+    def hidden_copy(d):
+        return remote(
+            hidden.at[row],
+            hidden.at[row],
+            hidden_send.at[d - 1],
+            hidden_recv.at[d - 1],
+            fsdp=(row + d) % prompts,
+        )
+
+    def hidden_came(d):
+        there = hidden.at[(row + prompts - d) % prompts]
+        return remote(
+            there,
+            there,
+            hidden_send.at[d - 1],
+            hidden_recv.at[d - 1],
+            fsdp=(row + d) % prompts,
+        )
+
+    for d in range(1, prompts):
+        hidden_copy(d).start()
+
+    sum_copy = remote(sum_out, sum_in, sum_send.at[0], sum_recv.at[0], tp=near)
+    half_copy = remote(half_out, half_in, sum_send.at[1], sum_recv.at[1], tp=far)
+
+    def project():
+        for d in range(1, prompts):
+            hidden_came(d).wait_recv()
+        connector_load.wait()
+        rows_in = hidden[...].reshape(prompts * QUERY_TOKENS, hidden.shape[2])
+        tile = HEAD_SIZE
+
+        @pl.loop(0, columns // tile)
+        def _(c):
+            at = pl.ds(pl.multiple_of(c * tile, tile), tile)
+            product = mm(rows_in, connector[:, at], NN)
+            partial[:, :, :, at] = product.reshape(prompts, size, block, tile)
+
+        for h in range(2):
+            sum_out[h] = partial[:, 2 * h + 1 - core].astype(bf)
+        sum_copy.start()
+
+    def halve():
+        sum_copy.wait_recv()
+        half[...] = partial[:, 2 * half_index + core] + sum_in[half_index].astype(jnp.float32)
+        other = 1 - half_index
+        half_out[...] = (partial[:, 2 * other + core] + sum_in[other].astype(jnp.float32)).astype(bf)
+        half_copy.start()
+
+    def token_copy(d):
+        to = (row + d) % prompts
+        return remote(
+            mine.at[to], context.at[me, row], token_send.at[d - 1], token_recv.at[d - 1], fsdp=to
+        )
+
+    def token_came(d):
+        there = context.at[me, (row + prompts - d) % prompts]
+        return remote(
+            there,
+            there,
+            token_send.at[d - 1],
+            token_recv.at[d - 1],
+            fsdp=(row + d) % prompts,
+        )
+
+    def spread():
+        half_copy.wait_recv()
+        mine[...] = (half[...] + half_in[...].astype(jnp.float32)).astype(bf)
+        context[me, row] = mine[row]
+        for d in range(1, prompts):
+            token_copy(d).start()
+
+    def gather_copy(k, who, to):
+        return remote(context.at[who], context.at[who], gather_send.at[k], gather_recv.at[k], tp=to)
+
+    def gather_far():
+        for d in range(1, prompts):
+            token_came(d).wait_recv()
+        gather_copy(0, me, far).start()
+        gather_copy(1, me, near).start()
+
+    def gather_near():
+        gather_copy(0, far, far).wait_recv()
+        gather_copy(2, far, near).start()
+
+    def gathered():
+        gather_copy(1, near, near).wait_recv()
+        gather_copy(2, peer_at(3), near).wait_recv()
+        g_load.wait()
+
+    def condition(position):
+        at = pl.ds(pl.multiple_of(position % columns, HEAD_SIZE), HEAD_SIZE)
+        return context[:, position // columns, :, at].reshape(QUERY_TOKENS, HEAD_SIZE)
+
+    def out_copy(i, which):
+        if which == 0:
+            source, target = latent.at[i], out_ref
+        else:
+            source, target = g_all.at[:, :, cols(i)], grad_ref
+        return pltpu.make_async_copy(source, target.at[0, :, :, cols(i)], out_sem.at[i, which])
+
+    def cross(i):
+        start = head_of(i) * HEAD_SIZE
+        out, grad, key_grad, value_gradient = cross_head(
+            latent[i].reshape(SAMPLE_COUNT * rows, HEAD_SIZE),
+            condition(start),
+            condition(heads * HEAD_SIZE + start),
+            g_all[:, :, cols(i)].reshape(SAMPLE_COUNT * rows, HEAD_SIZE),
+        )
+        latent[i] = out.reshape(SAMPLE_COUNT, rows, HEAD_SIZE)
+        g_all[:, :, cols(i)] = grad.reshape(SAMPLE_COUNT, rows, HEAD_SIZE)
+        out_copy(i, 0).start()
+        out_copy(i, 1).start()
+        pg[i % size, i // size, 0] = key_grad
+        pg[i % size, i // size, 1] = value_gradient
+
+    batches = ((0, per - 1), (per - 1, 1))
+
+    def pg_near_copy(b, h):
+        at = pl.ds(*batches[b])
+        return remote(
+            pg.at[2 * h + 1 - core, at],
+            pg_near.at[h, at],
+            pg_send.at[3 * b + h],
+            pg_recv.at[3 * b + h],
+            tp=near,
+        )
+
+    def pg_far_copy(b):
+        at = pl.ds(*batches[b])
+        return remote(
+            pg_out.at[at], pg_far.at[at], pg_send.at[3 * b + 2], pg_recv.at[3 * b + 2], tp=far
+        )
+
+    def pg_start(b):
+        for h in range(2):
+            pg_near_copy(b, h).start()
+
+    def pg_middle(b):
+        for h in range(2):
+            pg_near_copy(b, h).wait_recv()
+        at = pl.ds(*batches[b])
+        other = 1 - half_index
+        total = pg[2 * other + core, at].astype(jnp.float32) + pg_near[other, at].astype(jnp.float32)
+        pg_out[at] = total.astype(bf)
+        pg_far_copy(b).start()
+
+    def pg_end(b):
+        pg_far_copy(b).wait_recv()
+        first, count = batches[b]
+        for s in range(first, first + count):
+            total = (
+                pg[me, s].astype(jnp.float32)
+                + pg_near[half_index, s].astype(jnp.float32)
+                + pg_far[s].astype(jnp.float32)
+            )
+            context_grad_ref[0, :, :, s * HEAD_SIZE : (s + 1) * HEAD_SIZE] = total.astype(bf)
+
+    q_load.wait()
+    ready = heads * 15 // 24
+
+    @pl.loop(0, heads)
+    def _(i):
+        far_copy(i).wait_recv()
+        pass_copy(i).start()
+
+        @pl.when(i + DEPTH < heads)
+        def _():
+            far_copy(i + DEPTH).start()
+
+        near_copy(i).wait_recv()
+        for at, work in (
+            (heads * 4 // 24, project),
+            (heads * 5 // 24, halve),
+            (heads * 9 // 24, spread),
+            (heads * 10 // 24, gather_far),
+            (heads * 14 // 24, gather_near),
+            (ready, gathered),
+            (heads * 22 // 24, functools.partial(pg_middle, 0)),
+        ):
+            pl.when(i == at)(work)
+        pass_copy(i).wait_recv()
+
+        def part(which):
+            def of(sample):
+                return [kv[source, i, which, sample] for source in range(size)]
+
+            return of
+
+        pieces = self_head(lambda sample: q_all[sample, :, cols(i)], part(0), part(1))
+        for sample in range(SAMPLE_COUNT):
+            latent[i, sample] = pieces[sample]
+
+        first = jnp.where(i < ready, i + 1, jnp.where(i == ready, 0, i))
+
+        @pl.loop(first, i + 1)
+        def _(c):
+            cross(c)
+
+        @pl.when(i == size * (per - 1) - 1)
+        def _():
+            pg_start(0)
+
+    pg_start(1)
+    pg_end(0)
+    pg_middle(1)
+    pg_end(1)
+
+    @pl.loop(0, heads)
+    def _(i):
+        far_copy(i).wait_send()
+        near_copy(i).wait_send()
+        pass_copy(i).wait_send()
+        out_copy(i, 0).wait()
+        out_copy(i, 1).wait()
+
+    for d in range(1, size):
+        llm_copy(d).wait_send()
+    for d in range(1, prompts):
+        hidden_copy(d).wait_send()
+        token_copy(d).wait_send()
+    sum_copy.wait_send()
+    half_copy.wait_send()
+    gather_copy(0, me, far).wait_send()
+    gather_copy(1, me, near).wait_send()
+    gather_copy(2, far, near).wait_send()
+    for b in range(2):
+        for h in range(2):
+            pg_near_copy(b, h).wait_send()
+        pg_far_copy(b).wait_send()
+
+
+def whole_call(arrays):
+    llm_query, llm_kv, connector, self_query, self_key, latent_value, cotangent = arrays
+    size = lax.axis_size("tp")
+    prompts = lax.axis_size("fsdp")
+    heads = DENOISER_HEADS
+    per = heads // size
+    rows = self_query.shape[2]
+    block = QUERY_TOKENS // size
+    columns = connector.shape[1]
+    llm_width = llm_query.shape[2] // (LLM_HEADS // LLM_KV)
+    bf = jnp.bfloat16
+    dma = pltpu.SemaphoreType.DMA
+    width = heads * HEAD_SIZE
+    any_space = pl.BlockSpec(memory_space=pl.ANY)
+    token_block = (prompts, block, columns)
+    return pl.pallas_call(
+        functools.partial(whole_kernel, size, prompts),
+        in_specs=[any_space] * 7,
+        out_specs=[any_space, any_space, pl.BlockSpec(memory_space=pltpu.VMEM)],
+        out_shape=[
+            jax.ShapeDtypeStruct(self_query.shape, bf),
+            jax.ShapeDtypeStruct(self_query.shape, bf),
+            jax.ShapeDtypeStruct((1, 2, QUERY_TOKENS, per * HEAD_SIZE), bf),
+        ],
+        scratch_shapes=[
+            pltpu.VMEM((size, heads, 2, SAMPLE_COUNT, rows, HEAD_SIZE), bf),
+            pltpu.VMEM((SAMPLE_COUNT, rows, width), bf),
+            pltpu.VMEM((SAMPLE_COUNT, rows, width), bf),
+            pltpu.VMEM((heads, SAMPLE_COUNT, rows, HEAD_SIZE), bf),
+            pltpu.VMEM(llm_query.shape[1:], bf),
+            pltpu.VMEM((size, 2, llm_kv.shape[2], llm_width), bf),
+            pltpu.VMEM(connector.shape, bf),
+            pltpu.VMEM((prompts, QUERY_TOKENS, llm_query.shape[2]), bf),
+            pltpu.VMEM((prompts, size, block, columns), jnp.float32),
+            pltpu.VMEM((2,) + token_block, bf),
+            pltpu.VMEM((2,) + token_block, bf),
+            pltpu.VMEM(token_block, jnp.float32),
+            pltpu.VMEM(token_block, bf),
+            pltpu.VMEM(token_block, bf),
+            pltpu.VMEM(token_block, bf),
+            pltpu.VMEM((size,) + token_block, bf),
+            pltpu.VMEM((size, per, 2, QUERY_TOKENS, HEAD_SIZE), bf),
+            pltpu.VMEM((2, per, 2, QUERY_TOKENS, HEAD_SIZE), bf),
+            pltpu.VMEM((per, 2, QUERY_TOKENS, HEAD_SIZE), bf),
+            pltpu.VMEM((per, 2, QUERY_TOKENS, HEAD_SIZE), bf),
+            dma((heads, 2)),
+            dma((5,)),
+            dma((heads,)),
+            dma((heads,)),
+            dma((heads,)),
+            dma((heads,)),
+            dma((heads,)),
+            dma((heads,)),
+            dma((size - 1,)),
+            dma((size - 1,)),
+            dma((prompts - 1,)),
+            dma((prompts - 1,)),
+            dma((2,)),
+            dma((2,)),
+            dma((prompts - 1,)),
+            dma((prompts - 1,)),
+            dma((3,)),
+            dma((3,)),
+            dma((6,)),
+            dma((6,)),
+            dma((heads, 2)),
+        ],
+        compiler_params=pltpu.CompilerParams(
+            collective_id=0, has_side_effects=True, vmem_limit_bytes=60 * 1024 * 1024
+        ),
+        cost_estimate=pl.CostEstimate(
+            flops=10**10, bytes_accessed=23 * 10**6, transcendentals=10**7
+        ),
+    )(*arrays)
+
+
+def one_kernel_fits(connector):
+    size = lax.axis_size("tp")
+    return (
+        len(tp_masks()) == 2
+        and DENOISER_HEADS % size == 0
+        and LLM_KV % size == 0
+        and QUERY_TOKENS % (16 * size) == 0
+        and connector.shape[1] % HEAD_SIZE == 0
+    )
+
+
 def shards(llm_query, llm_kv, connector, self_query, self_key, latent_value, cotangent):
+    if one_kernel_fits(connector):
+        return whole_call(
+            (llm_query, llm_kv, connector, self_query, self_key, latent_value, cotangent)
+        )
     size = lax.axis_size("tp")
     groups = math.gcd(DENOISER_HEADS, size)
     masks = tp_masks()

time: 331 us -> 181 us (0.55)
  the two profiles are of different devices: /device:TPU:0 before, /device:TPU:13 now
where the time goes in v2:
time: 181 us
  Pallas kernels  174 us (96%)
  local copies, waits for them, and re-layouts  6.26 us (3%)
    pallas_call x1, Pallas kernels, whole_call(): pl.pallas_call(functools.partial(whole_kernel, size, prompts), in_specs=[...  174 us
    unnamed x7, local copies, waits for them, and re-layouts  6.26 us

profile of v2, /device:TPU:13, one launch (start us, length us, event | category | flops | bytes accessed | tf_op | source)
XLA Modules:
  0.0 181.2 jit_solution(13088983597678513757)
XLA Ops:
  0.6 174.3 %shard_map.94 = (bf16[1,2,256,3072]{3,2,1,0:T(8,128)(2,1)}, bf16[1,2,256,3072]{3,2,1,0:T(8,128)(2,1)}, bf16[1,2,64,768]{3,2,1,0:T(8,128)(2,1)}) custom-call(bf16[1,64,2048]{2,1,0:T(8,128)(2,1)} %llm_query_ref.1, bf16[1,2,80,1024]{3,2,1,0:T(8,128)(2,1)} %llm_kv_ref.1, bf16[2048,768]{1,0:T(8,128)(2,1)} %connector_ref.1, bf16[1,2,256,3072]{3,2,1,0:T(8,128)(2,1)} %query_ref.1, ...), custom_call_target="tpu_custom_call" | custom-call | flops 10000000000 | bytes 23000000 | tf_op jit(solution)/shard_map/pallas_call | solution.py:724
  175.0 0.0 copy-start
  175.0 3.9 %copy.13 = bf16[1,2,256,3072]{3,2,1,0:T(8,128)(2,1)} copy(bf16[1,2,256,3072]{3,2,1,0:T(8,128)(2,1)} %get-tuple-element.6) | data formatting | bytes 6291456
  178.9 0.0 copy-done
  178.9 0.0 copy-start.1
  178.9 1.7 copy.14
  180.5 0.0 copy-done.1
  180.5 0.7 copy.15
Async XLA Ops:
  175.0 3.9 %copy-start = (bf16[1,2,256,3072]{3,2,1,0:T(8,128)(2,1)S(1)}, bf16[1,2,256,3072]{3,2,1,0:T(8,128)(2,1)}, u32[]{:S(2)}) copy-start(bf16[1,2,256,3072]{3,2,1,0:T(8,128)(2,1)} %get-tuple-element.7) | copy-start | bytes 9437188
  178.9 1.7 copy-start.1

commit v3 on v2

--- a/solution.py
+++ b/solution.py
@@ -236,7 +236,8 @@
 
 
 MESH = pl.DeviceIdType.MESH
-DEPTH = 3
+DEPTH = 4
+STEPS = (6, 7, 11, 12, 16, 17)
 
 
 def self_head(query_of, keys_of, values_of):
@@ -633,7 +634,11 @@
             context_grad_ref[0, :, :, s * HEAD_SIZE : (s + 1) * HEAD_SIZE] = total.astype(bf)
 
     q_load.wait()
-    ready = heads * 15 // 24
+    ready = STEPS[5] * heads // 24
+    rate = -(-heads // (heads - ready - 1))
+    sent = next(
+        i for i in range(ready, heads) if min(rate * (i - ready + 1), i) >= size * (per - 1)
+    )
 
     @pl.loop(0, heads)
     def _(i):
@@ -645,16 +650,23 @@
             far_copy(i + DEPTH).start()
 
         near_copy(i).wait_recv()
-        for at, work in (
-            (heads * 4 // 24, project),
-            (heads * 5 // 24, halve),
-            (heads * 9 // 24, spread),
-            (heads * 10 // 24, gather_far),
-            (heads * 14 // 24, gather_near),
-            (ready, gathered),
-            (heads * 22 // 24, functools.partial(pg_middle, 0)),
-        ):
-            pl.when(i == at)(work)
+        works = (project, halve, spread, gather_far, gather_near, gathered)
+        for at, work in zip(STEPS, works):
+            pl.when(i == at * heads // 24)(work)
+        if sent + 1 < heads:
+            pl.when(i == sent + 1)(functools.partial(pg_middle, 0))
+
+        first = jnp.where(i < ready, i, jnp.minimum(rate * (i - ready), i - 1))
+        last = jnp.where(i < ready, i, jnp.minimum(rate * (i - ready + 1), i))
+
+        @pl.loop(first, last)
+        def _(c):
+            cross(c)
+
+        @pl.when(i == sent)
+        def _():
+            pg_start(0)
+
         pass_copy(i).wait_recv()
 
         def part(which):
@@ -667,16 +679,9 @@
         for sample in range(SAMPLE_COUNT):
             latent[i, sample] = pieces[sample]
 
-        first = jnp.where(i < ready, i + 1, jnp.where(i == ready, 0, i))
-
-        @pl.loop(first, i + 1)
-        def _(c):
-            cross(c)
-
-        @pl.when(i == size * (per - 1) - 1)
-        def _():
-            pg_start(0)
-
+    cross(heads - 1)
+    if sent + 1 >= heads:
+        pg_middle(0)
     pg_start(1)
     pg_end(0)
     pg_middle(1)

time: 181 us -> 174 us (0.961)
  the two profiles are of different devices: /device:TPU:13 before, /device:TPU:0 now
where the time goes in v3:
time: 174 us
  Pallas kernels  167 us (96%)
  local copies, waits for them, and re-layouts  6.26 us (4%)
    pallas_call x1, Pallas kernels, whole_call(): pl.pallas_call(functools.partial(whole_kernel, size, prompts), in_specs=[...  167 us
    unnamed x7, local copies, waits for them, and re-layouts  6.26 us

profile of v3, /device:TPU:0, one launch (start us, length us, event | category | flops | bytes accessed | tf_op | source)
XLA Modules:
  0.0 173.8 jit_solution(1047364927743850710)
XLA Ops:
  0.6 166.9 %shard_map.94 = (bf16[1,2,256,3072]{3,2,1,0:T(8,128)(2,1)}, bf16[1,2,256,3072]{3,2,1,0:T(8,128)(2,1)}, bf16[1,2,64,768]{3,2,1,0:T(8,128)(2,1)}) custom-call(bf16[1,64,2048]{2,1,0:T(8,128)(2,1)} %llm_query_ref.1, bf16[1,2,80,1024]{3,2,1,0:T(8,128)(2,1)} %llm_kv_ref.1, bf16[2048,768]{1,0:T(8,128)(2,1)} %connector_ref.1, bf16[1,2,256,3072]{3,2,1,0:T(8,128)(2,1)} %query_ref.1, ...), custom_call_target="tpu_custom_call" | custom-call | flops 10000000000 | bytes 23000000 | tf_op jit(solution)/shard_map/pallas_call | solution.py:729
  167.5 0.0 copy-start
  167.6 3.9 %copy.13 = bf16[1,2,256,3072]{3,2,1,0:T(8,128)(2,1)} copy(bf16[1,2,256,3072]{3,2,1,0:T(8,128)(2,1)} %get-tuple-element.6) | data formatting | bytes 6291456
  171.5 0.0 copy-done
  171.5 0.0 copy-start.1
  171.5 1.7 copy.14
  173.1 0.0 copy-done.1
  173.1 0.7 copy.15
Async XLA Ops:
  167.5 3.9 %copy-start = (bf16[1,2,256,3072]{3,2,1,0:T(8,128)(2,1)S(1)}, bf16[1,2,256,3072]{3,2,1,0:T(8,128)(2,1)}, u32[]{:S(2)}) copy-start(bf16[1,2,256,3072]{3,2,1,0:T(8,128)(2,1)} %get-tuple-element.7) | copy-start | bytes 9437188
  171.5 1.7 copy-start.1
